TPU v7x, 512 devices: a whole 4x8x8 slice. The times are simulated.
512 devices in a mesh: space: 64 (over z, y_hi, x), chaos: 8 (over y_lo, core).
Axes of the slice: x: 4, y: 8 (y_hi: 2, y_lo: 4; y = y_hi * 4 + y_lo), z: 8, core: 2. Of those that a mesh axis runs over, the one named last changes fastest.
Arguments:
- adjoint_field: bfloat16 [56, 32768], P('chaos', 'space'), may hold values from -6 to 6
- stiffness_tiles: bfloat16 [7, 256, 3, 128, 128], P(None, 'space'), may hold values from -0.3125 to 0.3125
- offsets: int32 [256, 3], P('space'), may hold values from -2 to 2, as said below
- galerkin: float32 [7, 56, 56], replicated, as said below
- adjoint_rhs: float32 [56, 32768], P('chaos', 'space'), may hold values from -6 to 6
Outputs:
- residual: float32 [56, 32768], P('chaos', 'space')
Inputs may be any that keep to these rules, and one draw needn't show every extreme that they name: offsets[r, 0] is 0 and the 3 entries of each row are distinct. Each galerkin[k] is symmetric.
All inputs are finite; a program needn't handle non-finite values.
Results may differ from a plain program's by a relative error of at most 0.0003.
Values may be sent and summed in bfloat16 or wider, within the bound.
No kernel may reach another device: no remote copies, remote signals or barrier semaphores. Data moves between devices by JAX's collectives and lax.ppermute only.
A program may use at most 64 MiB of HBM per device.

v0:
```python
import jax
import jax.numpy as jnp
from jax import lax
from jax.sharding import PartitionSpec as P


def from_behind(array, axis, by):
    peers = lax.axis_size(axis)
    pairs = [(i, i + by) for i in range(peers) if 0 <= i + by < peers]
    return lax.ppermute(array, axis, pairs)


def place_table(offsets, slot_count):
    tile_rows = offsets.shape[0]
    target = jnp.arange(tile_rows, dtype=jnp.int32)[:, None] + offsets + 2
    positions = jnp.arange(slot_count, dtype=jnp.int32)
    return (target[:, :, None] == positions[None, None, :]).astype(jnp.float32)


def tile_terms(blocks, stiffness_tiles, part_galerkin, placing):
    contrib = jnp.einsum(
        "prb,krsbc->krspc", blocks, stiffness_tiles, preferred_element_type=jnp.float32
    )
    combined = jnp.einsum(
        "kpq,krspc->qrsc", part_galerkin, contrib, precision=lax.Precision.HIGHEST
    )
    return jnp.einsum("rst,qrsc->qtc", placing, combined, precision=lax.Precision.HIGHEST)


def settle(extended):
    slot_count = extended.shape[1]
    interior = extended[:, 2 : slot_count - 2]
    tile_rows = interior.shape[1]
    from_below = from_behind(extended[:, slot_count - 2 :], "space", 1)
    from_above = from_behind(extended[:, :2], "space", -1)
    interior = interior.at[:, :2].add(from_below)
    interior = interior.at[:, tile_rows - 2 :].add(from_above)
    return interior


def body(adjoint_field, stiffness_tiles, offsets, galerkin, adjoint_rhs):
    tile_rows = stiffness_tiles.shape[1]
    tile_size = stiffness_tiles.shape[3]
    own_rows = adjoint_field.shape[0]
    placing = place_table(offsets, tile_rows + 4)
    first_row = lax.axis_index("chaos") * own_rows
    own_galerkin = lax.dynamic_slice_in_dim(galerkin, first_row, own_rows, 1)
    blocks = adjoint_field.reshape(own_rows, tile_rows, tile_size)
    extended = tile_terms(blocks, stiffness_tiles, own_galerkin, placing)
    extended = settle(extended)
    summed = lax.psum_scatter(extended, "chaos", scatter_dimension=0, tiled=True)
    applied = summed.reshape(own_rows, tile_rows * tile_size)
    return adjoint_rhs - applied


def solution(mesh):
    return jax.shard_map(
        body,
        mesh=mesh,
        in_specs=(
            P("chaos", "space"),
            P(None, "space", None, None, None),
            P("space", None),
            P(),
            P("chaos", "space"),
        ),
        out_specs=P("chaos", "space"),
        check_vma=False,
    )
```

profile of v0, /device:TPU:57, one launch (start us, length us, event | category | flops | bytes accessed | tf_op | source)
XLA Modules:
  0.0 115.7 jit_solution(18308056942424074448)
XLA Ops:
  6.5 0.0 copy-start
  6.5 0.0 all-reduce.3.cloned.1.call-start
  6.5 0.7 add_add_fusion
  7.3 0.1 copy.11
  7.4 0.0 copy-start.2
  7.4 2.3 %fusion.2 = f32[7,4,3,7,128]{4,3,2,0,1:T(8,128)S(1)} fusion(bf16[7,4,3,128,128]{4,3,2,1,0:T(8,128)(2,1)} %param.10, bf16[7,512]{1,0:T(8,128)(2,1)} %param.9), kind=kOutput, calls=%fused_computation.2 | convolution fusion | flops 19267584 | bytes 3060736 | tf_op jit(solution)/shard_map/prb,krsbc->krspc/dot_general | solution.py:21
  9.6 0.0 copy-done
  9.6 0.5 convolution_bitcast_fusion
  10.2 0.4 convolution_bitcast_fusion.1
  10.7 3.1 %collective-permute-start = (f32[56,2,128]{2,1,0:T(2,128)S(1)}, f32[56,2,128]{2,1,0:T(2,128)S(1)}, u32[]{:S(2)}, u32[]{:S(2)}) collective-permute-start(f32[56,2,128]{2,1,0:T(2,128)S(1)} %get-tuple-element.30), channel_id=1, source_target_pairs={{0,8},{8,16},{16,24},{24,32},{32,40},{40,48},{48,56},{56,64},{64,7... | collective-permute-start | bytes 172040 | tf_op jit(solution)/shard_map/ppermute | solution.py:10
  13.8 8.2 %collective-permute-start.1 = (f32[56,2,128]{2,1,0:T(2,128)S(1)}, f32[56,2,128]{2,1,0:T(2,128)S(1)}, u32[]{:S(2)}, u32[]{:S(2)}) collective-permute-start(f32[56,2,128]{2,1,0:T(2,128)S(1)} %get-tuple-element.29), channel_id=1, source_target_pairs={{8,0},{16,8},{24,16},{32,24},{40,32},{48,40},{56,48},{64,56},{72,6... | collective-permute-start | bytes 172040 | tf_op jit(solution)/shard_map/ppermute | solution.py:10
  22.0 0.0 collective-permute-done
  22.0 0.1 fusion.7
  22.1 1.1 collective-permute-done.1
  23.2 0.1 fusion.6
  23.3 0.0 copy-start.1
  23.3 0.6 copy-done.1
  23.9 0.0 all-reduce.3.cloned.1.call-update
  24.0 1.3 %dynamic-slice.16 = u32[1]{0:T(128)} dynamic-slice(u32[512]{0:T(512)} %constant.71, u32[]{:T(128)S(6)} %add.37), dynamic_slice_sizes={1} | dynamic-slice | bytes 12
  25.9 81.7 %all-reduce.3.cloned.1.call-done = f32[56,4,128]{2,1,0:T(4,128)} async-done(((f32[56,4,128]{2,1,0:T(4,128)}), f32[56,4,128]{2,1,0:T(4,128)}) %all-reduce.3.cloned.1.call-update) | async-done | bytes 114704
  107.5 0.7 dynamic-slice_bitcast_fusion
  108.3 0.0 copy-done.2
  108.3 0.6 bitcast_subtract_fusion
  (2 shorter events, 0.1 us)
Async XLA Ops:
  6.5 3.1 %copy-start = (f32[7,56,56]{2,1,0:T(8,128)S(1)}, f32[7,56,56]{2,1,0:T(8,128)}, u32[]{:S(2)}) copy-start(f32[7,56,56]{2,1,0:T(8,128)} %param.12) | copy-start | bytes 263428
  6.5 101.0 %all-reduce.3.cloned.1.call-start = ((), (), s32[]{:S(2)}) async-start(), calls=%async_computation | async-start | bytes 229376
  7.4 100.9 %copy-start.2 = (f32[7,512]{1,0:T(8,128)S(1)}, f32[7,512]{1,0:T(8,128)}, u32[]{:S(2)}) copy-start(f32[7,512]{1,0:T(8,128)} %param.13) | copy-start | bytes 43012
  10.7 11.4 %collective-permute-start = (f32[56,2,128]{2,1,0:T(2,128)S(1)}, f32[56,2,128]{2,1,0:T(2,128)S(1)}, u32[]{:S(2)}, u32[]{:S(2)}) collective-permute-start(f32[56,2,128]{2,1,0:T(2,128)S(1)} %get-tuple-element.30), channel_id=1, source_target_pairs={{0,8},{8,16},{16,24},{24,32},{32,40},{40,48},{48,56},{56,64},{64,7... | collective-permute-start | bytes 172040 | tf_op jit(solution)/shard_map/ppermute | solution.py:10
  13.8 9.4 %collective-permute-start.1 = (f32[56,2,128]{2,1,0:T(2,128)S(1)}, f32[56,2,128]{2,1,0:T(2,128)S(1)}, u32[]{:S(2)}, u32[]{:S(2)}) collective-permute-start(f32[56,2,128]{2,1,0:T(2,128)S(1)} %get-tuple-element.29), channel_id=1, source_target_pairs={{8,0},{16,8},{24,16},{32,24},{40,32},{48,40},{56,48},{64,56},{72,6... | collective-permute-start | bytes 172040 | tf_op jit(solution)/shard_map/ppermute | solution.py:10
  23.3 0.6 copy-start.1
Sparse Core Ops, SparseCore 0:
  24.1 83.4 all-reduce.2
where the time goes:
time: 116 us
  waiting for transfers between devices  82.8 us (71%)
  between operations  14.1 us (12%)
  starting transfers between devices  11.3 us (10%)
  matrix products  3.24 us (3%)
  local copies, waits for them, and re-layouts  2.78 us (2%)
  other arithmetic  1.46 us (1%)
    unnamed x2, waiting for transfers between devices  81.7 us
    ppermute x2, starting transfers between devices, from_behind(): return lax.ppermute(array, axis, pairs)  11.3 us
    unnamed x8, local copies, waits for them, and re-layouts  2.62 us
  transfers between devices with their start and end apart: 3, of which 2 were waited for; matrix products, arithmetic and copies ran while one was open for 1% of the time, Pallas kernels for 0%

commit v1 on v0

v1 whole, which is shorter than its diff:
```python
import jax
import jax.numpy as jnp
from jax import lax
from jax.experimental import pallas as pl
from jax.experimental.pallas import tpu as pltpu
from jax.sharding import PartitionSpec as P

ROWS = 8
REACH = 2


def split(x):
    high = x.astype(jnp.bfloat16)
    low = (x - high.astype(jnp.float32)).astype(jnp.bfloat16)
    return high, low


def tiles_kernel(
    where_ref, offsets_ref, field_ref, tiles_ref, galerkin_ref, rhs_ref,
    main_ref, first_ref, second_ref, gathered, mixer, slots,
):
    terms, tile_rows, near, size, _ = tiles_ref.shape
    groups, own, dofs = field_ref.shape
    chaos = groups * own
    space, far_first = where_ref[0], where_ref[2]
    for g in range(groups):
        gathered[g * own : (g + 1) * own, :] = field_ref[g].astype(jnp.float32)
    field = gathered[...].astype(jnp.bfloat16)
    mixer[...] = jnp.zeros_like(mixer)
    for b in range(2):
        start = where_ref[1 + 2 * b] * own
        for k in range(terms):
            mixer[b, k, :own, :] = galerkin_ref[k, pl.ds(start, own), :]
    mix_high, mix_low = split(mixer[...].reshape(2 * terms * ROWS, chaos))
    mixed = jnp.dot(mix_high, field, preferred_element_type=jnp.float32)
    mixed += jnp.dot(mix_low, field, preferred_element_type=jnp.float32)
    mixed = mixed.reshape(2, terms, ROWS, dofs)
    high = mixed.astype(jnp.bfloat16).astype(jnp.float32)
    parts = jnp.concatenate([high[0:1], mixed[0:1] - high[0:1], high[1:2], mixed[1:2] - high[1:2]], axis=0)
    slots[...] = jnp.zeros_like(slots)
    for r in range(tile_rows):
        left = jnp.concatenate(
            [parts[:, k, :, r * size : (r + 1) * size].reshape(4 * ROWS, size) for k in range(terms)],
            axis=1,
        ).astype(jnp.bfloat16)
        right = jnp.concatenate(
            [tiles_ref[:, r, s].reshape(terms * size, size) for s in range(near)], axis=1
        )
        product = jnp.dot(left, right, preferred_element_type=jnp.float32)
        product = product.reshape(2, 2, ROWS, near * size)
        product = (product[:, 0] + product[:, 1]).reshape(2 * ROWS, near * size)
        for s in range(near):
            slot = r + REACH + offsets_ref[r, s]
            slots[slot] += product[:, s * size : (s + 1) * size]
    for t in range(tile_rows):
        main_ref[:, t * size : (t + 1) * size] = (
            rhs_ref[:, t * size : (t + 1) * size] - slots[t + REACH, :own]
        )
    even = lax.rem(space, 2) == 0
    for t in range(REACH):
        low_a, low_b = slots[t, :ROWS], slots[t, ROWS:]
        top_a, top_b = slots[tile_rows + REACH + t, :ROWS], slots[tile_rows + REACH + t, ROWS:]
        columns = slice(t * size, (t + 1) * size)
        far = jnp.where(even, low_b, top_b)
        near_by = jnp.where(even, low_a, top_a)
        first_ref[:, columns] = jnp.where(far_first == 1, far, near_by)
        second_ref[:, columns] = jnp.where(even, top_a, low_a)


def body(adjoint_field, stiffness_tiles, offsets, galerkin, adjoint_rhs):
    terms, tile_rows, near, size, _ = stiffness_tiles.shape
    own, dofs = adjoint_field.shape
    groups, slabs = lax.axis_size("chaos"), lax.axis_size("space")
    chaos = own * groups
    row = 4
    turn = groups // 2
    space, block = lax.axis_index("space"), lax.axis_index("chaos")
    at_end = ((space % row) == 0) | ((space % row) == row - 1)
    other = jnp.bitwise_xor(block, turn)
    where = jnp.stack([space, block, at_end.astype(jnp.int32), other]).astype(jnp.int32)

    copies = jnp.broadcast_to(adjoint_field[None], (groups, own, dofs))
    field = lax.all_to_all(copies, "chaos", 0, 0)

    halo = REACH * size
    smem = pl.BlockSpec(memory_space=pltpu.SMEM)
    vmem = pl.BlockSpec(memory_space=pltpu.VMEM)
    main, first, second = pl.pallas_call(
        tiles_kernel,
        out_shape=(
            jax.ShapeDtypeStruct((own, dofs), jnp.float32),
            jax.ShapeDtypeStruct((ROWS, halo), jnp.float32),
            jax.ShapeDtypeStruct((ROWS, halo), jnp.float32),
        ),
        in_specs=[smem, smem, vmem, vmem, vmem, vmem],
        out_specs=(vmem, vmem, vmem),
        scratch_shapes=[
            pltpu.VMEM((chaos, dofs), jnp.float32),
            pltpu.VMEM((2, terms, ROWS, chaos), jnp.float32),
            pltpu.VMEM((tile_rows + 2 * REACH, 2 * ROWS, size), jnp.float32),
        ],
        compiler_params=pltpu.CompilerParams(vmem_limit_bytes=32 * 1024 * 1024),
    )(where, offsets, field, stiffness_tiles, galerkin, adjoint_rhs)

    def swaps(parity):
        pairs = []
        for s in range(parity, slabs - 1, 2):
            for c in range(groups):
                d = c ^ turn if s % row == row - 1 else c
                pairs += [(s * groups + c, (s + 1) * groups + d), ((s + 1) * groups + d, s * groups + c)]
        return pairs

    got_first = lax.ppermute(first, ("space", "chaos"), swaps(1))
    got_second = lax.ppermute(second, ("space", "chaos"), swaps(0))
    even = (space % 2) == 0
    got = jnp.where(
        even,
        jnp.concatenate([got_first, got_second], axis=1),
        jnp.concatenate([got_second, got_first], axis=1),
    )
    return main - got[:own]


def solution(mesh):
    return jax.shard_map(
        body,
        mesh=mesh,
        in_specs=(
            P("chaos", "space"),
            P(None, "space", None, None, None),
            P("space", None),
            P(),
            P("chaos", "space"),
        ),
        out_specs=P("chaos", "space"),
        check_vma=False,
    )
```

time: 116 us -> 30.5 us (0.26)
  the two profiles are of different devices: /device:TPU:57 before, /device:TPU:448 now
where the time goes in v1:
time: 30.5 us; the launch traced here: 30.1 us
  starting transfers between devices  13.2 us (43%)
  waiting for transfers between devices  9.45 us (31%)
  local copies, waits for them, and re-layouts  5.43 us (18%)
  Pallas kernels  1.26 us (4%)
  other arithmetic  0.69 us (2%)
    ppermute x1, starting transfers between devices, body(): got_first = lax.ppermute(first, ('space', 'chaos'), swaps(1))  6.44 us
    all_to_all x1, waiting for transfers between devices, body(): field = lax.all_to_all(copies, 'chaos', 0, 0)  5.84 us
    all_to_all x1, starting transfers between devices, body(): field = lax.all_to_all(copies, 'chaos', 0, 0)  4.88 us
    unnamed x8, local copies, waits for them, and re-layouts  4.1 us
    ppermute x1, waiting for transfers between devices, body(): got_first = lax.ppermute(first, ('space', 'chaos'), swaps(1))  2.27 us
    ppermute x1, starting transfers between devices, body(): got_second = lax.ppermute(second, ('space', 'chaos'), swaps(0))  1.92 us
    broadcast_in_dim x1, local copies, waits for them, and re-layouts, body(): copies = jnp.broadcast_to(adjoint_field[None], (groups, own, dofs))  1.33 us
    ppermute x1, waiting for transfers between devices, body(): got_second = lax.ppermute(second, ('space', 'chaos'), swaps(0))  1.33 us
  transfers between devices with their start and end apart: 3, of which 3 were waited for; matrix products, arithmetic and copies ran while one was open for 0% of the time, Pallas kernels for 0%

profile of v1, /device:TPU:448, one launch (start us, length us, event | category | flops | bytes accessed | tf_op | source)
XLA Modules:
  0.0 30.1 jit_solution(7627950302422354190)
XLA Ops:
  0.0 1.3 %broadcast_in_dim.2 = bf16[8,7,512]{2,1,0:T(8,128)(2,1)} broadcast(bf16[7,512]{1,0:T(8,128)(2,1)} %param.5), dimensions={1,2} | broadcast | bytes 64512 | tf_op jit(solution)/shard_map/broadcast_in_dim | solution.py:82
  1.3 4.9 %all-to-all-start = ((bf16[8,7,512]{2,1,0:T(8,128)(2,1)}), bf16[8,7,512]{2,1,0:T(8,128)(2,1)S(1)}, u32[]{:S(2)}, u32[]{:S(2)}) async-start(bf16[8,7,512]{2,1,0:T(8,128)(2,1)} %broadcast_in_dim.2), calls=%async_computation | async-start | bytes 131072 | tf_op jit(solution)/shard_map/all_to_all | solution.py:83
  6.2 0.1 pad_add_fusion.where_ref
  6.3 5.8 %all-to-all-done.field_ref = bf16[8,7,512]{2,1,0:T(8,128)(2,1)S(1)} async-done(((bf16[8,7,512]{2,1,0:T(8,128)(2,1)}), bf16[8,7,512]{2,1,0:T(8,128)(2,1)S(1)}, u32[]{:S(2)}, u32[]{:S(2)}) %all-to-all-start) | async-done | bytes 57376 | tf_op jit(solution)/shard_map/all_to_all | solution.py:83
  12.1 0.0 copy-start
  12.1 1.8 %copy-done = bf16[7,4,3,128,128]{4,3,2,1,0:T(8,128)(2,1)S(1)} copy-done((bf16[7,4,3,128,128]{4,3,2,1,0:T(8,128)(2,1)S(1)}, bf16[7,4,3,128,128]{4,3,2,1,0:T(8,128)(2,1)}, u32[]{:S(2)}) %copy-start) | copy-done | bytes 2752536
  13.9 0.0 copy-start.1
  13.9 0.9 %copy-done.1 = f32[7,56,56]{2,1,0:T(8,128)S(1)} copy-done((f32[7,56,56]{2,1,0:T(8,128)S(1)}, f32[7,56,56]{2,1,0:T(8,128)}, u32[]{:S(2)}) %copy-start.1) | copy-done | bytes 87832
  14.8 0.0 copy-start.2
  14.8 0.7 %copy-done.2 = f32[7,512]{1,0:T(8,128)S(1)} copy-done((f32[7,512]{1,0:T(8,128)S(1)}, f32[7,512]{1,0:T(8,128)}, u32[]{:S(2)}) %copy-start.2) | copy-done | bytes 14360
  15.6 0.0 copy-start.3
  15.6 0.7 %copy-done.3 = s32[4,3]{1,0:T(4,128)S(1)} copy-done((s32[4,3]{1,0:T(4,128)S(1)}, s32[4,3]{1,0:T(4,128)}, u32[]{:S(2)}) %copy-start.3) | copy-done | bytes 72
  16.2 1.3 %shard_map.55 = (f32[7,512]{1,0:T(8,128)S(1)}, f32[8,256]{1,0:T(8,128)S(1)}, f32[8,256]{1,0:T(8,128)S(1)}) custom-call(s32[4]{0:T(128)S(1)} %pad_add_fusion.where_ref, s32[4,3]{1,0:T(4,128)S(1)} %copy-done.3, bf16[8,7,512]{2,1,0:T(8,128)(2,1)S(1)} %all-to-all-done.field_ref, bf16[7,4,3,128,128]{4,3,2,1,0:T(8,128)(2,1)S(1)} %copy-done, ...), custom_call_target="tpu_custom_call" | custom-call | tf_op jit(solution)/shard_map/pallas_call | solution.py:88
  17.5 6.4 %collective-permute-start = (f32[8,256]{1,0:T(8,128)S(1)}, f32[8,256]{1,0:T(8,128)S(1)}, u32[]{:S(2)}, u32[]{:S(2)}) collective-permute-start(f32[8,256]{1,0:T(8,128)S(1)} %get-tuple-element.9), channel_id=1, source_target_pairs={{8,16},{16,8},{9,17},{17,9},{10,18},{18,10},{11,19},{19,11},{12,20... | collective-permute-start | bytes 24584 | tf_op jit(solution)/shard_map/ppermute | solution.py:113
  24.0 1.9 %collective-permute-start.1 = (f32[8,256]{1,0:T(8,128)S(1)}, f32[8,256]{1,0:T(8,128)S(1)}, u32[]{:S(2)}, u32[]{:S(2)}) collective-permute-start(f32[8,256]{1,0:T(8,128)S(1)} %get-tuple-element.10), channel_id=1, source_target_pairs={{0,8},{8,0},{1,9},{9,1},{2,10},{10,2},{3,11},{11,3},{4,12},{12,4},... | collective-permute-start | bytes 24584 | tf_op jit(solution)/shard_map/ppermute | solution.py:114
  25.9 2.3 %collective-permute-done = f32[8,256]{1,0:T(8,128)S(1)} collective-permute-done((f32[8,256]{1,0:T(8,128)S(1)}, f32[8,256]{1,0:T(8,128)S(1)}, u32[]{:S(2)}, u32[]{:S(2)}) %collective-permute-start) | collective-permute-done | bytes 8224 | tf_op jit(solution)/shard_map/ppermute | solution.py:113
  28.2 1.3 %collective-permute-done.1 = f32[8,256]{1,0:T(8,128)S(1)} collective-permute-done((f32[8,256]{1,0:T(8,128)S(1)}, f32[8,256]{1,0:T(8,128)S(1)}, u32[]{:S(2)}, u32[]{:S(2)}) %collective-permute-start.1) | collective-permute-done | bytes 8224 | tf_op jit(solution)/shard_map/ppermute | solution.py:114
  29.5 0.6 %fusion.1 = f32[7,512]{1,0:T(8,128)} fusion(f32[7,512]{1,0:T(8,128)S(1)} %get-tuple-element.8, f32[8,256]{1,0:T(8,128)S(1)} %collective-permute-done.1, f32[8,256]{1,0:T(8,128)S(1)} %collective-permute-done, pred[]{:T(512)S(6)} %eq.15), kind=kLoop, calls=%fused_computation.2 | loop fusion | flops 14336 | bytes 45057 | tf_op jit(solution)/shard_map/sub | solution.py:121
Async XLA Ops:
  1.3 10.8 %all-to-all-start = ((bf16[8,7,512]{2,1,0:T(8,128)(2,1)}), bf16[8,7,512]{2,1,0:T(8,128)(2,1)S(1)}, u32[]{:S(2)}, u32[]{:S(2)}) async-start(bf16[8,7,512]{2,1,0:T(8,128)(2,1)} %broadcast_in_dim.2), calls=%async_computation | async-start | bytes 131072 | tf_op jit(solution)/shard_map/all_to_all | solution.py:83
  12.1 1.8 %copy-start = (bf16[7,4,3,128,128]{4,3,2,1,0:T(8,128)(2,1)S(1)}, bf16[7,4,3,128,128]{4,3,2,1,0:T(8,128)(2,1)}, u32[]{:S(2)}) copy-start(bf16[7,4,3,128,128]{4,3,2,1,0:T(8,128)(2,1)} %tiles_ref.1) | copy-start | bytes 8257540
  13.9 0.9 %copy-start.1 = (f32[7,56,56]{2,1,0:T(8,128)S(1)}, f32[7,56,56]{2,1,0:T(8,128)}, u32[]{:S(2)}) copy-start(f32[7,56,56]{2,1,0:T(8,128)} %galerkin_ref.1) | copy-start | bytes 263428
  14.8 0.7 %copy-start.2 = (f32[7,512]{1,0:T(8,128)S(1)}, f32[7,512]{1,0:T(8,128)}, u32[]{:S(2)}) copy-start(f32[7,512]{1,0:T(8,128)} %rhs_ref.1) | copy-start | bytes 43012
  15.6 0.7 %copy-start.3 = (s32[4,3]{1,0:T(4,128)S(1)}, s32[4,3]{1,0:T(4,128)}, u32[]{:S(2)}) copy-start(s32[4,3]{1,0:T(4,128)} %offsets_ref.1) | copy-start | bytes 148
  17.5 10.7 %collective-permute-start = (f32[8,256]{1,0:T(8,128)S(1)}, f32[8,256]{1,0:T(8,128)S(1)}, u32[]{:S(2)}, u32[]{:S(2)}) collective-permute-start(f32[8,256]{1,0:T(8,128)S(1)} %get-tuple-element.9), channel_id=1, source_target_pairs={{8,16},{16,8},{9,17},{17,9},{10,18},{18,10},{11,19},{19,11},{12,20... | collective-permute-start | bytes 24584 | tf_op jit(solution)/shard_map/ppermute | solution.py:113
  24.0 5.5 %collective-permute-start.1 = (f32[8,256]{1,0:T(8,128)S(1)}, f32[8,256]{1,0:T(8,128)S(1)}, u32[]{:S(2)}, u32[]{:S(2)}) collective-permute-start(f32[8,256]{1,0:T(8,128)S(1)} %get-tuple-element.10), channel_id=1, source_target_pairs={{0,8},{8,0},{1,9},{9,1},{2,10},{10,2},{3,11},{11,3},{4,12},{12,4},... | collective-permute-start | bytes 24584 | tf_op jit(solution)/shard_map/ppermute | solution.py:114

commit v2 on v1

v2 whole, which is shorter than its diff:
```python
import jax
import jax.numpy as jnp
from jax import lax
from jax.experimental import pallas as pl
from jax.experimental.pallas import tpu as pltpu
from jax.sharding import PartitionSpec as P

ROWS = 8
REACH = 2
SPAN = 2 * REACH + 1
RUN = 4


def split(x):
    high = x.astype(jnp.bfloat16)
    low = (x - high.astype(jnp.float32)).astype(jnp.bfloat16)
    return high, low


def in_hbm(x):
    return pltpu.with_memory_space_constraint(x, pltpu.HBM)


def stage_kernel(
    offsets_ref, tiles_ref, galerkin_ref, rhs_ref,
    tiles_out, mixer_out, masks_out, rhs_out, galerkin, mixer, sems,
):
    terms, tile_rows, near, _, _ = tiles_ref.shape
    own = rhs_ref.shape[0]
    groups = galerkin_ref.shape[1] // own
    moves = [
        pltpu.make_async_copy(galerkin_ref, galerkin, sems.at[0]),
        pltpu.make_async_copy(rhs_ref, rhs_out, sems.at[1]),
    ]
    for k in range(terms):
        moves.append(pltpu.make_async_copy(tiles_ref.at[k], tiles_out.at[k], sems.at[2 + k]))
    for move in moves:
        move.start()
    space, block = lax.axis_index("space"), lax.axis_index("chaos")
    def row_of(flag):
        return jnp.full((1, masks_out.shape[1]), flag.astype(jnp.float32))
    for r in range(tile_rows):
        for s in range(near):
            for o in range(SPAN):
                at = (r * near + s) * SPAN + o
                masks_out[at : at + 1, :] = row_of(offsets_ref[r, s] == o - REACH)
    at = tile_rows * near * SPAN
    place = lax.rem(space, RUN)
    masks_out[at : at + 1, :] = row_of(lax.rem(space, 2) == 0)
    masks_out[at + 1 : at + 2, :] = row_of(jnp.logical_or(place == 0, place == RUN - 1))
    mixer[...] = jnp.zeros_like(mixer)
    moves[0].wait()
    half = groups // 2
    other = jnp.where(block < half, block + half, block - half)
    for b, owner in enumerate((block, other)):
        for k in range(terms):
            mixer[b, k, :own, :] = galerkin[k, pl.ds(owner * own, own), :]
    high, low = split(mixer[...].reshape(2 * terms * ROWS, groups * own))
    mixer_out[0], mixer_out[1] = high, low
    for move in moves[1:]:
        move.wait()


def tiles_kernel(
    field_ref, tiles_ref, mixer_ref, masks_ref, rhs_ref,
    main_ref, first_ref, second_ref, gathered,
):
    terms, tile_rows, near, size, _ = tiles_ref.shape
    groups, own, dofs = field_ref.shape
    for g in range(groups):
        gathered[g * own : (g + 1) * own, :] = field_ref[g].astype(jnp.float32)
    field = gathered[...].astype(jnp.bfloat16)
    mixed = jnp.dot(mixer_ref[0], field, preferred_element_type=jnp.float32)
    mixed += jnp.dot(mixer_ref[1], field, preferred_element_type=jnp.float32)
    mixed = mixed.reshape(2, terms, ROWS, dofs)
    high = mixed.astype(jnp.bfloat16).astype(jnp.float32)
    low = mixed - high
    slots = [jnp.zeros((2 * ROWS, size), jnp.float32) for _ in range(tile_rows + 2 * REACH)]
    for r in range(tile_rows):
        columns = slice(r * size, (r + 1) * size)
        left = jnp.concatenate(
            [
                jnp.concatenate([part[b, k, :, columns] for b in range(2) for part in (high, low)], axis=0)
                for k in range(terms)
            ],
            axis=1,
        ).astype(jnp.bfloat16)
        right = jnp.concatenate(
            [tiles_ref[:, r, s].reshape(terms * size, size) for s in range(near)], axis=1
        )
        product = jnp.dot(left, right, preferred_element_type=jnp.float32)
        product = product.reshape(2, 2, ROWS, near * size)
        product = (product[:, 0] + product[:, 1]).reshape(2 * ROWS, near * size)
        slots[r + REACH] += product[:, :size]
        for s in range(1, near):
            entry = product[:, s * size : (s + 1) * size]
            for o in range(SPAN):
                if o == REACH:
                    continue
                at = (r * near + s) * SPAN + o
                slots[r + o] += jnp.where(masks_ref[at : at + 1, :] > 0, entry, 0.0)
    for t in range(tile_rows):
        columns = slice(t * size, (t + 1) * size)
        main_ref[:, columns] = rhs_ref[:, columns] - slots[t + REACH][:own]
    at = tile_rows * near * SPAN
    even = masks_ref[at : at + 1, :] > 0
    far = masks_ref[at + 1 : at + 2, :] > 0
    for t in range(REACH):
        bottom, top = slots[t], slots[tile_rows + REACH + t]
        columns = slice(t * size, (t + 1) * size)
        across = jnp.where(even, bottom, top)
        first_ref[:, columns] = jnp.where(far, across[ROWS:], across[:ROWS])
        second_ref[:, columns] = jnp.where(even, top[:ROWS], bottom[:ROWS])


def body(adjoint_field, stiffness_tiles, offsets, galerkin, adjoint_rhs):
    terms, tile_rows, near, size, _ = stiffness_tiles.shape
    own, dofs = adjoint_field.shape
    groups, slabs = lax.axis_size("chaos"), lax.axis_size("space")
    chaos = own * groups
    turn = groups // 2
    smem = pl.BlockSpec(memory_space=pltpu.SMEM)
    vmem = pl.BlockSpec(memory_space=pltpu.VMEM)
    hbm = pl.BlockSpec(memory_space=pltpu.HBM)
    limit = 24 * 1024 * 1024

    copies = jnp.broadcast_to(adjoint_field[None], (groups, own, dofs))
    field = lax.all_to_all(copies, "chaos", 0, 0)

    n_masks = tile_rows * near * SPAN + 2
    n_masks += -n_masks % 8
    tiles, mixer, masks, rhs = pl.pallas_call(
        stage_kernel,
        out_shape=(
            jax.ShapeDtypeStruct(stiffness_tiles.shape, jnp.bfloat16),
            jax.ShapeDtypeStruct((2, 2 * terms * ROWS, chaos), jnp.bfloat16),
            jax.ShapeDtypeStruct((n_masks, size), jnp.float32),
            jax.ShapeDtypeStruct((own, dofs), jnp.float32),
        ),
        in_specs=[smem, hbm, hbm, hbm],
        out_specs=(vmem, vmem, vmem, vmem),
        scratch_shapes=[
            pltpu.VMEM((terms, chaos, chaos), jnp.float32),
            pltpu.VMEM((2, terms, ROWS, chaos), jnp.float32),
            pltpu.SemaphoreType.DMA((2 + terms,)),
        ],
        compiler_params=pltpu.CompilerParams(vmem_limit_bytes=limit),
        cost_estimate=pl.CostEstimate(flops=0, bytes_accessed=6 * 2**20, transcendentals=0),
    )(offsets, in_hbm(stiffness_tiles), in_hbm(galerkin), in_hbm(adjoint_rhs))

    halo = REACH * size
    main, first, second = pl.pallas_call(
        tiles_kernel,
        out_shape=(
            jax.ShapeDtypeStruct((own, dofs), jnp.float32),
            jax.ShapeDtypeStruct((ROWS, halo), jnp.float32),
            jax.ShapeDtypeStruct((ROWS, halo), jnp.float32),
        ),
        in_specs=[vmem] * 5,
        out_specs=(vmem, vmem, vmem),
        scratch_shapes=[pltpu.VMEM((chaos, dofs), jnp.float32)],
        compiler_params=pltpu.CompilerParams(vmem_limit_bytes=limit),
    )(field, tiles, mixer, masks, rhs)

    def partner(s, c):
        return (s + 1) * groups + (c ^ turn if s % RUN == RUN - 1 else c)

    pairs = [(s * groups + c, partner(s, c), s) for s in range(slabs - 1) for c in range(groups)]
    axes = ("space", "chaos")
    out = [(b, a) if s % RUN == 0 else (a, b) for a, b, s in pairs if s % 2 == 0]
    both = [pair for a, b, s in pairs if s % 2 == 1 for pair in ((a, b), (b, a))]
    back = [(b, a) for a, b in out]
    swap = out + back
    got_first = lax.ppermute(first, axes, both)
    got_second = lax.ppermute(second, axes, swap)
    even = (lax.axis_index("space") % 2) == 0
    halo_a = jnp.where(even, got_first, got_second)
    halo_b = jnp.where(even, got_second, got_first)
    got = jnp.concatenate([halo_a, halo_b], axis=1)
    return main - got[:own]


def solution(mesh):
    return jax.shard_map(
        body,
        mesh=mesh,
        in_specs=(
            P("chaos", "space"),
            P(None, "space", None, None, None),
            P("space", None),
            P(),
            P("chaos", "space"),
        ),
        out_specs=P("chaos", "space"),
        check_vma=False,
    )
```

time: 30.5 us -> 25.7 us (0.84)
  local copies, waits for them, and re-layouts: 5.43 us -> 2 us
  waiting for transfers between devices: 9.45 us -> 6.36 us
  Pallas kernels: 1.26 us -> 3.15 us
    unnamed x8 -> x2, local copies, waits for them, and re-layouts: 4.1 us -> 0.68 us
    all_to_all x1, waiting for transfers between devices: 5.84 us -> 2.75 us  [body(): field = lax.all_to_all(copies, 'chaos', 0, 0)]
    pallas_call x0 -> x1, Pallas kernels: none -> 2.47 us  [body(): pl.pallas_call(stage_kernel, out_shape=(jax.ShapeDtypeStruct(stiffness_ti...]
    pallas_call x1, Pallas kernels: 1.26 us -> 0.68 us  [body(): pl.pallas_call(tiles_kernel, out_shape=(jax.ShapeDtypeStruct((own, dofs),...]
  transfers between devices with their start and end apart: 3 -> 3, of which waited for: 3 -> 3; matrix products, arithmetic and copies ran while one was open for 0% -> 0% of each run, Pallas kernels for 0% -> 10%
where the time goes in v2:
time: 25.7 us; the launch traced here: 25.4 us
  starting transfers between devices  13.2 us (51%)
  waiting for transfers between devices  6.36 us (25%)
  Pallas kernels  3.15 us (12%)
  local copies, waits for them, and re-layouts  2 us (8%)
  other arithmetic  0.62 us (2%)
    ppermute x1, starting transfers between devices, body(): got_first = lax.ppermute(first, axes, both)  6.44 us
    all_to_all x1, starting transfers between devices, body(): field = lax.all_to_all(copies, 'chaos', 0, 0)  4.88 us
    all_to_all x1, waiting for transfers between devices, body(): field = lax.all_to_all(copies, 'chaos', 0, 0)  2.75 us
    pallas_call x1, Pallas kernels, body(): pl.pallas_call(stage_kernel, out_shape=(jax.ShapeDtypeStruct(stiffness_ti...  2.47 us
    ppermute x1, waiting for transfers between devices, body(): got_first = lax.ppermute(first, axes, both)  2.27 us
    ppermute x1, starting transfers between devices, body(): got_second = lax.ppermute(second, axes, swap)  1.92 us
    ppermute x1, waiting for transfers between devices, body(): got_second = lax.ppermute(second, axes, swap)  1.33 us
    broadcast_in_dim x1, local copies, waits for them, and re-layouts, body(): copies = jnp.broadcast_to(adjoint_field[None], (groups, own, dofs))  1.32 us
  transfers between devices with their start and end apart: 3, of which 3 were waited for; matrix products, arithmetic and copies ran while one was open for 0% of the time, Pallas kernels for 10%

profile of v2, /device:TPU:448, one launch (start us, length us, event | category | flops | bytes accessed | tf_op | source)
XLA Modules:
  0.0 25.4 jit_solution(14881028853911867843)
XLA Ops:
  0.0 1.3 %broadcast_in_dim.2 = bf16[8,7,512]{2,1,0:T(8,128)(2,1)} broadcast(bf16[7,512]{1,0:T(8,128)(2,1)} %param.5), dimensions={1,2} | broadcast | bytes 64512 | tf_op jit(solution)/shard_map/broadcast_in_dim | solution.py:127
  1.3 4.9 %all-to-all-start = ((bf16[8,7,512]{2,1,0:T(8,128)(2,1)}), bf16[8,7,512]{2,1,0:T(8,128)(2,1)S(1)}, u32[]{:S(2)}, u32[]{:S(2)}) async-start(bf16[8,7,512]{2,1,0:T(8,128)(2,1)} %broadcast_in_dim.2), calls=%async_computation | async-start | bytes 131072 | tf_op jit(solution)/shard_map/all_to_all | solution.py:128
  6.2 0.0 copy-start
  6.2 0.7 %copy-done = s32[4,3]{1,0:T(4,128)S(1)} copy-done((s32[4,3]{1,0:T(4,128)S(1)}, s32[4,3]{1,0:T(4,128)}, u32[]{:S(2)}) %copy-start) | copy-done | bytes 72
  6.9 2.5 %shard_map.55 = (bf16[7,4,3,128,128]{4,3,2,1,0:T(8,128)(2,1)S(1)}, bf16[2,112,56]{2,1,0:T(8,128)(2,1)S(1)}, f32[64,128]{1,0:T(8,128)S(1)}, f32[7,512]{1,0:T(8,128)S(1)}) custom-call(s32[4,3]{1,0:T(4,128)S(1)} %copy-done, bf16[7,4,3,128,128]{4,3,2,1,0:T(8,128)(2,1)} %tiles_ref.1, f32[7,56,56]{2,1,0:T(8,128)} %galerkin_ref.1, f32[7,512]{1,0:T(8,128)} %rhs_ref.1), custom_call_target="tpu_custom_call" | custom-call | bytes 6291456 | tf_op jit(solution)/shard_map/pallas_call | solution.py:132
  9.4 2.8 %all-to-all-done.field_ref = bf16[8,7,512]{2,1,0:T(8,128)(2,1)S(1)} async-done(((bf16[8,7,512]{2,1,0:T(8,128)(2,1)}), bf16[8,7,512]{2,1,0:T(8,128)(2,1)S(1)}, u32[]{:S(2)}, u32[]{:S(2)}) %all-to-all-start) | async-done | bytes 57376 | tf_op jit(solution)/shard_map/all_to_all | solution.py:128
  12.1 0.7 %shard_map.56 = (f32[7,512]{1,0:T(8,128)S(1)}, f32[8,256]{1,0:T(8,128)S(1)}, f32[8,256]{1,0:T(8,128)S(1)}) custom-call(bf16[8,7,512]{2,1,0:T(8,128)(2,1)S(1)} %all-to-all-done.field_ref, bf16[7,4,3,128,128]{4,3,2,1,0:T(8,128)(2,1)S(1)} %get-tuple-element.12.tiles_ref, bf16[2,112,56]{2,1,0:T(8,128)(2,1)S(1)} %get-tuple-element.13.mixer_ref, ...), custom_call_target="tpu_custom_call" | custom-call | tf_op jit(solution)/shard_map/pallas_call | solution.py:152
  12.8 6.4 %collective-permute-start = (f32[8,256]{1,0:T(8,128)S(1)}, f32[8,256]{1,0:T(8,128)S(1)}, u32[]{:S(2)}, u32[]{:S(2)}) collective-permute-start(f32[8,256]{1,0:T(8,128)S(1)} %get-tuple-element.17), channel_id=1, source_target_pairs={{8,16},{16,8},{9,17},{17,9},{10,18},{18,10},{11,19},{19,11},{12,20... | collective-permute-start | bytes 24584 | tf_op jit(solution)/shard_map/ppermute | solution.py:174
  19.3 1.9 %collective-permute-start.1 = (f32[8,256]{1,0:T(8,128)S(1)}, f32[8,256]{1,0:T(8,128)S(1)}, u32[]{:S(2)}, u32[]{:S(2)}) collective-permute-start(f32[8,256]{1,0:T(8,128)S(1)} %get-tuple-element.18), channel_id=1, source_target_pairs={{8,0},{9,1},{10,2},{11,3},{12,4},{13,5},{14,6},{15,7},{16,24},{17,... | collective-permute-start | bytes 24584 | tf_op jit(solution)/shard_map/ppermute | solution.py:175
  21.2 2.3 %collective-permute-done = f32[8,256]{1,0:T(8,128)S(1)} collective-permute-done((f32[8,256]{1,0:T(8,128)S(1)}, f32[8,256]{1,0:T(8,128)S(1)}, u32[]{:S(2)}, u32[]{:S(2)}) %collective-permute-start) | collective-permute-done | bytes 8224 | tf_op jit(solution)/shard_map/ppermute | solution.py:174
  23.5 1.3 %collective-permute-done.1 = f32[8,256]{1,0:T(8,128)S(1)} collective-permute-done((f32[8,256]{1,0:T(8,128)S(1)}, f32[8,256]{1,0:T(8,128)S(1)}, u32[]{:S(2)}, u32[]{:S(2)}) %collective-permute-start.1) | collective-permute-done | bytes 8224 | tf_op jit(solution)/shard_map/ppermute | solution.py:175
  24.8 0.6 %fusion = f32[7,512]{1,0:T(8,128)} fusion(f32[7,512]{1,0:T(8,128)S(1)} %get-tuple-element.16, f32[8,256]{1,0:T(8,128)S(1)} %get-tuple-element.20, f32[8,256]{1,0:T(8,128)S(1)} %get-tuple-element.19), kind=kLoop, calls=%fused_computation.1 | loop fusion | flops 7168 | bytes 45056 | tf_op jit(solution)/shard_map/sub | solution.py:180
  (1 shorter events, 0.0 us)
Async XLA Ops:
  1.3 10.8 %all-to-all-start = ((bf16[8,7,512]{2,1,0:T(8,128)(2,1)}), bf16[8,7,512]{2,1,0:T(8,128)(2,1)S(1)}, u32[]{:S(2)}, u32[]{:S(2)}) async-start(bf16[8,7,512]{2,1,0:T(8,128)(2,1)} %broadcast_in_dim.2), calls=%async_computation | async-start | bytes 131072 | tf_op jit(solution)/shard_map/all_to_all | solution.py:128
  6.2 0.7 %copy-start = (s32[4,3]{1,0:T(4,128)S(1)}, s32[4,3]{1,0:T(4,128)}, u32[]{:S(2)}) copy-start(s32[4,3]{1,0:T(4,128)} %offsets_ref.1) | copy-start | bytes 148
  12.8 10.7 %collective-permute-start = (f32[8,256]{1,0:T(8,128)S(1)}, f32[8,256]{1,0:T(8,128)S(1)}, u32[]{:S(2)}, u32[]{:S(2)}) collective-permute-start(f32[8,256]{1,0:T(8,128)S(1)} %get-tuple-element.17), channel_id=1, source_target_pairs={{8,16},{16,8},{9,17},{17,9},{10,18},{18,10},{11,19},{19,11},{12,20... | collective-permute-start | bytes 24584 | tf_op jit(solution)/shard_map/ppermute | solution.py:174
  19.3 5.5 %collective-permute-start.1 = (f32[8,256]{1,0:T(8,128)S(1)}, f32[8,256]{1,0:T(8,128)S(1)}, u32[]{:S(2)}, u32[]{:S(2)}) collective-permute-start(f32[8,256]{1,0:T(8,128)S(1)} %get-tuple-element.18), channel_id=1, source_target_pairs={{8,0},{9,1},{10,2},{11,3},{12,4},{13,5},{14,6},{15,7},{16,24},{17,... | collective-permute-start | bytes 24584 | tf_op jit(solution)/shard_map/ppermute | solution.py:175

commit v3 on v2

v3 whole, which is shorter than its diff:
```python
import jax
import jax.numpy as jnp
from jax import lax
from jax.experimental import pallas as pl
from jax.experimental.pallas import tpu as pltpu
from jax.sharding import PartitionSpec as P

ROWS = 8
REACH = 2
SPAN = 2 * REACH + 1
RUN = 4


def in_hbm(x):
    return pltpu.with_memory_space_constraint(x, pltpu.HBM)


def split(x):
    high = x.astype(jnp.bfloat16)
    low = (x - high.astype(jnp.float32)).astype(jnp.bfloat16)
    return high, low


def stage_kernel(
    field_ref, offsets_ref, tiles_ref, galerkin_ref,
    copies_out, tiles_out, mixer_out, masks_out,
    field, offsets, galerkin, mixer, sems,
):
    terms, tile_rows, near, _, _ = tiles_ref.shape
    groups, own, _ = copies_out.shape
    pairs = [(field_ref, field), (galerkin_ref, galerkin), (offsets_ref, offsets)]
    pairs.append((tiles_ref.at[:, :, 1:near], tiles_out))
    moves = [pltpu.make_async_copy(a, b, sems.at[i]) for i, (a, b) in enumerate(pairs)]
    for move in moves:
        move.start()
    space, block = lax.axis_index("space"), lax.axis_index("chaos")
    moves[0].wait()
    value = field[...]
    for g in range(groups):
        copies_out[g] = value
    mixer[...] = jnp.zeros_like(mixer)
    moves[1].wait()
    half = groups // 2
    other = jnp.where(block < half, block + half, block - half)
    for b, owner in enumerate((block, other)):
        for k in range(terms):
            mixer[b, k, :own, :] = galerkin[k, pl.ds(owner * own, own), :]
    high, low = split(mixer[...].reshape(2 * terms * ROWS, groups * own))
    mixer_out[0], mixer_out[1] = high, low
    moves[2].wait()

    def row_of(flag):
        return jnp.full((1, masks_out.shape[1]), flag.astype(jnp.float32))

    for r in range(tile_rows):
        for s in range(1, near):
            for o in range(SPAN):
                at = (r * near + s) * SPAN + o
                masks_out[at : at + 1, :] = row_of(offsets[r, s] == o - REACH)
    at = tile_rows * near * SPAN
    place = lax.rem(space, RUN)
    masks_out[at : at + 1, :] = row_of(lax.rem(space, 2) == 0)
    masks_out[at + 1 : at + 2, :] = row_of(jnp.logical_or(place == 0, place == RUN - 1))
    moves[3].wait()


def mix(field_ref, mixer_ref, gathered, blocks):
    groups, own, dofs = field_ref.shape
    rows = mixer_ref.shape[1] // 2 * blocks
    for g in range(groups):
        gathered[g * own : (g + 1) * own, :] = field_ref[g].astype(jnp.float32)
    field = gathered[...].astype(jnp.bfloat16)
    mixed = jnp.dot(mixer_ref[0, :rows], field, preferred_element_type=jnp.float32)
    mixed += jnp.dot(mixer_ref[1, :rows], field, preferred_element_type=jnp.float32)
    mixed = mixed.reshape(blocks, rows // blocks // ROWS, ROWS, dofs)
    high = mixed.astype(jnp.bfloat16).astype(jnp.float32)
    return high, mixed - high


def times_tiles(parts, columns, right):
    blocks, terms = parts[0].shape[:2]
    left = jnp.concatenate(
        [
            jnp.concatenate([part[b, k, :, columns] for b in range(blocks) for part in parts], axis=0)
            for k in range(terms)
        ],
        axis=1,
    ).astype(jnp.bfloat16)
    product = jnp.dot(left, right, preferred_element_type=jnp.float32)
    product = product.reshape(blocks, 2, ROWS, right.shape[1])
    return (product[:, 0] + product[:, 1]).reshape(blocks * ROWS, right.shape[1])


def halo_kernel(
    field_ref, tiles_ref, mixer_ref, masks_ref,
    first_ref, second_ref, inner_ref, gathered,
):
    terms, tile_rows, others, size, _ = tiles_ref.shape
    parts = mix(field_ref, mixer_ref, gathered, 2)
    slots = [jnp.zeros((2 * ROWS, size), jnp.float32) for _ in range(tile_rows + 2 * REACH)]
    for r in range(tile_rows):
        right = jnp.concatenate(
            [tiles_ref[:, r, s].reshape(terms * size, size) for s in range(others)], axis=1
        )
        product = times_tiles(parts, slice(r * size, (r + 1) * size), right)
        for s in range(others):
            entry = product[:, s * size : (s + 1) * size]
            for o in range(SPAN):
                if o == REACH:
                    continue
                at = (r * (others + 1) + s + 1) * SPAN + o
                slots[r + o] += jnp.where(masks_ref[at : at + 1, :] > 0, entry, 0.0)
    at = tile_rows * (others + 1) * SPAN
    even = masks_ref[at : at + 1, :] > 0
    far = masks_ref[at + 1 : at + 2, :] > 0
    for t in range(REACH):
        bottom, top = slots[t], slots[tile_rows + REACH + t]
        columns = slice(t * size, (t + 1) * size)
        across = jnp.where(even, bottom, top)
        first_ref[:, columns] = jnp.where(far, across[ROWS:], across[:ROWS])
        second_ref[:, columns] = jnp.where(even, top[:ROWS], bottom[:ROWS])
    for t in range(tile_rows):
        inner_ref[:, t * size : (t + 1) * size] = slots[t + REACH][:ROWS]


def inner_kernel(
    field_ref, tiles_ref, mixer_ref, inner_ref, rhs_ref,
    main_ref, tiles, rhs, gathered, sems,
):
    terms, tile_rows, _, size, _ = tiles_ref.shape
    own = field_ref.shape[1]
    get_tiles = pltpu.make_async_copy(tiles_ref.at[:, :, 0], tiles, sems.at[0])
    get_rhs = pltpu.make_async_copy(rhs_ref, rhs, sems.at[1])
    get_tiles.start()
    get_rhs.start()
    parts = mix(field_ref, mixer_ref, gathered, 1)
    get_tiles.wait()
    get_rhs.wait()
    for r in range(tile_rows):
        columns = slice(r * size, (r + 1) * size)
        product = times_tiles(parts, columns, tiles[:, r].reshape(terms * size, size))
        main_ref[:, columns] = rhs[:, columns] - (inner_ref[:, columns] + product)[:own]


def body(adjoint_field, stiffness_tiles, offsets, galerkin, adjoint_rhs):
    terms, tile_rows, near, size, _ = stiffness_tiles.shape
    own, dofs = adjoint_field.shape
    groups, slabs = lax.axis_size("chaos"), lax.axis_size("space")
    chaos = own * groups
    turn = groups // 2
    vmem = pl.BlockSpec(memory_space=pltpu.VMEM)
    hbm = pl.BlockSpec(memory_space=pltpu.HBM)
    params = pltpu.CompilerParams(vmem_limit_bytes=24 * 1024 * 1024)
    all_tiles, rhs = in_hbm(stiffness_tiles), in_hbm(adjoint_rhs)

    n_masks = tile_rows * near * SPAN + 2
    n_masks += -n_masks % 8
    copies, tiles, mixer, masks = pl.pallas_call(
        stage_kernel,
        out_shape=(
            jax.ShapeDtypeStruct((groups, own, dofs), jnp.bfloat16),
            jax.ShapeDtypeStruct((terms, tile_rows, near - 1, size, size), jnp.bfloat16),
            jax.ShapeDtypeStruct((2, 2 * terms * ROWS, chaos), jnp.bfloat16),
            jax.ShapeDtypeStruct((n_masks, size), jnp.float32),
        ),
        in_specs=[hbm] * 4,
        out_specs=(vmem,) * 4,
        scratch_shapes=[
            pltpu.VMEM((own, dofs), jnp.bfloat16),
            pltpu.SMEM(offsets.shape, jnp.int32),
            pltpu.VMEM((terms, chaos, chaos), jnp.float32),
            pltpu.VMEM((2, terms, ROWS, chaos), jnp.float32),
            pltpu.SemaphoreType.DMA((4,)),
        ],
        compiler_params=params,
    )(in_hbm(adjoint_field), in_hbm(offsets), all_tiles, in_hbm(galerkin))

    field = lax.all_to_all(copies, "chaos", 0, 0)

    halo = REACH * size
    first, second, inner = pl.pallas_call(
        halo_kernel,
        out_shape=(
            jax.ShapeDtypeStruct((ROWS, halo), jnp.float32),
            jax.ShapeDtypeStruct((ROWS, halo), jnp.float32),
            jax.ShapeDtypeStruct((ROWS, dofs), jnp.float32),
        ),
        in_specs=[vmem] * 4,
        out_specs=(vmem,) * 3,
        scratch_shapes=[pltpu.VMEM((chaos, dofs), jnp.float32)],
        compiler_params=params,
    )(field, tiles, mixer, masks)

    main = pl.pallas_call(
        inner_kernel,
        out_shape=jax.ShapeDtypeStruct((own, dofs), jnp.float32),
        in_specs=[vmem, hbm, vmem, vmem, hbm],
        out_specs=vmem,
        scratch_shapes=[
            pltpu.VMEM((terms, tile_rows, size, size), jnp.bfloat16),
            pltpu.VMEM((own, dofs), jnp.float32),
            pltpu.VMEM((chaos, dofs), jnp.float32),
            pltpu.SemaphoreType.DMA((2,)),
        ],
        compiler_params=params,
    )(field, all_tiles, mixer, inner, rhs)

    def partner(s, c):
        return (s + 1) * groups + (c ^ turn if s % RUN == RUN - 1 else c)

    pairs = [(s * groups + c, partner(s, c), s) for s in range(slabs - 1) for c in range(groups)]
    axes = ("space", "chaos")

    def swap(x, parity):
        return lax.ppermute(x, axes, [p for a, b, s in pairs if s % 2 == parity for p in ((a, b), (b, a))])

    got_first, got_second = swap(first, 1), swap(second, 0)
    even = (lax.axis_index("space") % 2) == 0
    halo_a = jnp.where(even, got_first, got_second)
    halo_b = jnp.where(even, got_second, got_first)
    got = jnp.concatenate([halo_a, halo_b], axis=1)
    return main - got[:own]


def solution(mesh):
    return jax.shard_map(
        body,
        mesh=mesh,
        in_specs=(
            P("chaos", "space"),
            P(None, "space", None, None, None),
            P("space", None),
            P(),
            P("chaos", "space"),
        ),
        out_specs=P("chaos", "space"),
        check_vma=False,
    )
```

time: 25.7 us -> 25.6 us (level)
  the two profiles are of different devices: /device:TPU:448 before, /device:TPU:256 now
where the time goes in v3:
time: 25.6 us; the launch traced here: 25.3 us
  blocking collectives  10.6 us (41%)
  starting transfers between devices  6.8 us (27%)
  Pallas kernels  3.71 us (14%)
  waiting for transfers between devices  3.56 us (14%)
  other arithmetic  0.62 us (2%)
    all_to_all x1, blocking collectives, body(): field = lax.all_to_all(copies, 'chaos', 0, 0)  10.6 us
    ppermute x2, starting transfers between devices, swap(): lax.ppermute(x, axes, [p for a, b, s in pairs if s % 2 == parity for p in...  6.8 us
    ppermute x2, waiting for transfers between devices, swap(): lax.ppermute(x, axes, [p for a, b, s in pairs if s % 2 == parity for p in...  3.56 us
    pallas_call x1, Pallas kernels, body(): pl.pallas_call(stage_kernel, out_shape=(jax.ShapeDtypeStruct((groups, own...  1.67 us
    pallas_call x1, Pallas kernels, body(): pl.pallas_call(inner_kernel, out_shape=jax.ShapeDtypeStruct((own, dofs),...  1.48 us
    sub x1, other arithmetic, body(): return main - got[:own]  0.61 us
    pallas_call x1, Pallas kernels, body(): pl.pallas_call(halo_kernel, out_shape=(jax.ShapeDtypeStruct((ROWS, halo),...  0.56 us
  transfers between devices with their start and end apart: 2, of which 1 were waited for; matrix products, arithmetic and copies ran while one was open for 0% of the time, Pallas kernels for 6%

profile of v3, /device:TPU:256, one launch (start us, length us, event | category | flops | bytes accessed | tf_op | source)
XLA Modules:
  0.0 25.3 jit_solution(11645861157934965752)
XLA Ops:
  0.0 1.7 %shard_map.55 = (bf16[8,7,512]{2,1,0:T(8,128)(2,1)S(1)}, bf16[7,4,2,128,128]{4,3,2,1,0:T(8,128)(2,1)S(1)}, bf16[2,112,56]{2,1,0:T(8,128)(2,1)S(1)}, f32[64,128]{1,0:T(8,128)S(1)}) custom-call(bf16[7,512]{1,0:T(8,128)(2,1)} %field_ref.1, s32[4,3]{1,0:T(4,128)} %offsets_ref.1, bf16[7,4,3,128,128]{4,3,2,1,0:T(8,128)(2,1)} %tiles_ref.3, f32[7,56,56]{2,1,0:T(8,128)} %galerkin_ref.1), custom_call_target="tpu_custom_call" | custom-call | tf_op jit(solution)/shard_map/pallas_call | solution.py:158
  1.7 10.6 %all_to_all.5.field_ref = bf16[8,7,512]{2,1,0:T(8,128)(2,1)S(1)} all-to-all(bf16[8,7,512]{2,1,0:T(8,128)(2,1)S(1)} %get-tuple-element.12), channel_id=1, replica_groups=mesh['space'=64,'chaos'=8] {'chaos'}, dimensions={0} | all-to-all | bytes 114688 | tf_op jit(solution)/shard_map/all_to_all | solution.py:178
  12.3 0.6 %shard_map.56 = (f32[8,256]{1,0:T(8,128)S(1)}, f32[8,256]{1,0:T(8,128)S(1)}, f32[8,512]{1,0:T(8,128)S(1)}) custom-call(bf16[8,7,512]{2,1,0:T(8,128)(2,1)S(1)} %all_to_all.5.field_ref, bf16[7,4,2,128,128]{4,3,2,1,0:T(8,128)(2,1)S(1)} %get-tuple-element.14.tiles_ref, bf16[2,112,56]{2,1,0:T(8,128)(2,1)S(1)} %get-tuple-element.13.mixer_ref, ...), custom_call_target="tpu_custom_call" | custom-call | tf_op jit(solution)/shard_map/pallas_call | solution.py:181
  12.8 4.8 %collective-permute-start = (f32[8,256]{1,0:T(8,128)S(1)}, f32[8,256]{1,0:T(8,128)S(1)}, u32[]{:S(2)}, u32[]{:S(2)}) collective-permute-start(f32[8,256]{1,0:T(8,128)S(1)} %get-tuple-element.17), channel_id=1, source_target_pairs={{8,16},{16,8},{9,17},{17,9},{10,18},{18,10},{11,19},{19,11},{12,20... | collective-permute-start | bytes 24584 | tf_op jit(solution)/shard_map/ppermute | solution.py:215
  17.7 2.0 %collective-permute-start.1 = (f32[8,256]{1,0:T(8,128)S(1)}, f32[8,256]{1,0:T(8,128)S(1)}, u32[]{:S(2)}, u32[]{:S(2)}) collective-permute-start(f32[8,256]{1,0:T(8,128)S(1)} %get-tuple-element.18), channel_id=1, source_target_pairs={{0,8},{8,0},{1,9},{9,1},{2,10},{10,2},{3,11},{11,3},{4,12},{12,4},... | collective-permute-start | bytes 24584 | tf_op jit(solution)/shard_map/ppermute | solution.py:215
  19.7 1.5 %shard_map.57 = f32[7,512]{1,0:T(8,128)S(1)} custom-call(bf16[8,7,512]{2,1,0:T(8,128)(2,1)S(1)} %all_to_all.5.field_ref, bf16[7,4,3,128,128]{4,3,2,1,0:T(8,128)(2,1)} %tiles_ref.3, bf16[2,112,56]{2,1,0:T(8,128)(2,1)S(1)} %get-tuple-element.13.mixer_ref, f32[8,512]{1,0:T(8,128)S(1)} %get-tuple-element.16.inner_ref, f32[7,512]{1,0:T(8,128)} %rhs_ref.1), custom_call_target="tpu_custom_call" | custom-call | tf_op jit(solution)/shard_map/pallas_call | solution.py:194
  21.2 3.6 %collective-permute-done = f32[8,256]{1,0:T(8,128)S(1)} collective-permute-done((f32[8,256]{1,0:T(8,128)S(1)}, f32[8,256]{1,0:T(8,128)S(1)}, u32[]{:S(2)}, u32[]{:S(2)}) %collective-permute-start) | collective-permute-done | bytes 8224 | tf_op jit(solution)/shard_map/ppermute | solution.py:215
  24.7 0.0 collective-permute-done.1
  24.7 0.6 %fusion = f32[7,512]{1,0:T(8,128)} fusion(f32[7,512]{1,0:T(8,128)S(1)} %shard_map.57, f32[8,256]{1,0:T(8,128)S(1)} %get-tuple-element.20, f32[8,256]{1,0:T(8,128)S(1)} %get-tuple-element.19), kind=kLoop, calls=%fused_computation.1 | loop fusion | flops 7168 | bytes 45056 | tf_op jit(solution)/shard_map/sub | solution.py:222
  (1 shorter events, 0.0 us)
Async XLA Ops:
  12.8 11.9 %collective-permute-start = (f32[8,256]{1,0:T(8,128)S(1)}, f32[8,256]{1,0:T(8,128)S(1)}, u32[]{:S(2)}, u32[]{:S(2)}) collective-permute-start(f32[8,256]{1,0:T(8,128)S(1)} %get-tuple-element.17), channel_id=1, source_target_pairs={{8,16},{16,8},{9,17},{17,9},{10,18},{18,10},{11,19},{19,11},{12,20... | collective-permute-start | bytes 24584 | tf_op jit(solution)/shard_map/ppermute | solution.py:215
  17.7 7.0 %collective-permute-start.1 = (f32[8,256]{1,0:T(8,128)S(1)}, f32[8,256]{1,0:T(8,128)S(1)}, u32[]{:S(2)}, u32[]{:S(2)}) collective-permute-start(f32[8,256]{1,0:T(8,128)S(1)} %get-tuple-element.18), channel_id=1, source_target_pairs={{0,8},{8,0},{1,9},{9,1},{2,10},{10,2},{3,11},{11,3},{4,12},{12,4},... | collective-permute-start | bytes 24584 | tf_op jit(solution)/shard_map/ppermute | solution.py:215

commit v4 on v3

--- a/solution.py
+++ b/solution.py
@@ -9,6 +9,7 @@
 REACH = 2
 SPAN = 2 * REACH + 1
 RUN = 4
+BLOCKS = 3
 
 
 def in_hbm(x):
@@ -41,11 +42,12 @@
     mixer[...] = jnp.zeros_like(mixer)
     moves[1].wait()
     half = groups // 2
-    other = jnp.where(block < half, block + half, block - half)
-    for b, owner in enumerate((block, other)):
+    near_by = block + 1 - 2 * lax.rem(block, 2)
+    far_off = jnp.where(near_by < half, near_by + half, near_by - half)
+    for b, owner in enumerate((near_by, far_off, block)):
         for k in range(terms):
             mixer[b, k, :own, :] = galerkin[k, pl.ds(owner * own, own), :]
-    high, low = split(mixer[...].reshape(2 * terms * ROWS, groups * own))
+    high, low = split(mixer[...].reshape(BLOCKS * terms * ROWS, groups * own))
     mixer_out[0], mixer_out[1] = high, low
     moves[2].wait()
 
@@ -64,17 +66,36 @@
     moves[3].wait()
 
 
-def mix(field_ref, mixer_ref, gathered, blocks):
+def mix(field_ref, mixer_ref, gathered, first, blocks):
     groups, own, dofs = field_ref.shape
-    rows = mixer_ref.shape[1] // 2 * blocks
+    rows = mixer_ref.shape[1] // BLOCKS
     for g in range(groups):
         gathered[g * own : (g + 1) * own, :] = field_ref[g].astype(jnp.float32)
     field = gathered[...].astype(jnp.bfloat16)
-    mixed = jnp.dot(mixer_ref[0, :rows], field, preferred_element_type=jnp.float32)
-    mixed += jnp.dot(mixer_ref[1, :rows], field, preferred_element_type=jnp.float32)
-    mixed = mixed.reshape(blocks, rows // blocks // ROWS, ROWS, dofs)
+    used = slice(first * rows, (first + blocks) * rows)
+    mixed = jnp.dot(mixer_ref[0, used], field, preferred_element_type=jnp.float32)
+    mixed += jnp.dot(mixer_ref[1, used], field, preferred_element_type=jnp.float32)
+    mixed = mixed.reshape(blocks, rows // ROWS, ROWS, dofs)
     high = mixed.astype(jnp.bfloat16).astype(jnp.float32)
     return high, mixed - high
+
+
+def beside(tiles_ref, r):
+    terms, _, others, size, _ = tiles_ref.shape
+    return jnp.concatenate(
+        [tiles_ref[:, r, s].reshape(terms * size, size) for s in range(others)], axis=1
+    )
+
+
+def add_entries(slots, product, masks_ref, r, others, wanted):
+    size = masks_ref.shape[1]
+    for s in range(others):
+        entry = product[:, s * size : (s + 1) * size]
+        for o in range(SPAN):
+            if o == REACH or r + o not in wanted:
+                continue
+            at = (r * (others + 1) + s + 1) * SPAN + o
+            slots[r + o] += jnp.where(masks_ref[at : at + 1, :] > 0, entry, 0.0)
 
 
 def times_tiles(parts, columns, right):
@@ -93,23 +114,15 @@
 
 def halo_kernel(
     field_ref, tiles_ref, mixer_ref, masks_ref,
-    first_ref, second_ref, inner_ref, gathered,
+    first_ref, second_ref, gathered,
 ):
-    terms, tile_rows, others, size, _ = tiles_ref.shape
-    parts = mix(field_ref, mixer_ref, gathered, 2)
-    slots = [jnp.zeros((2 * ROWS, size), jnp.float32) for _ in range(tile_rows + 2 * REACH)]
-    for r in range(tile_rows):
-        right = jnp.concatenate(
-            [tiles_ref[:, r, s].reshape(terms * size, size) for s in range(others)], axis=1
-        )
-        product = times_tiles(parts, slice(r * size, (r + 1) * size), right)
-        for s in range(others):
-            entry = product[:, s * size : (s + 1) * size]
-            for o in range(SPAN):
-                if o == REACH:
-                    continue
-                at = (r * (others + 1) + s + 1) * SPAN + o
-                slots[r + o] += jnp.where(masks_ref[at : at + 1, :] > 0, entry, 0.0)
+    _, tile_rows, others, size, _ = tiles_ref.shape
+    parts = mix(field_ref, mixer_ref, gathered, 0, 2)
+    wanted = [*range(REACH), *range(tile_rows + REACH, tile_rows + 2 * REACH)]
+    slots = {t: jnp.zeros((2 * ROWS, size), jnp.float32) for t in wanted}
+    for r in range(tile_rows):
+        product = times_tiles(parts, slice(r * size, (r + 1) * size), beside(tiles_ref, r))
+        add_entries(slots, product, masks_ref, r, others, wanted)
     at = tile_rows * (others + 1) * SPAN
     even = masks_ref[at : at + 1, :] > 0
     far = masks_ref[at + 1 : at + 2, :] > 0
@@ -119,27 +132,30 @@
         across = jnp.where(even, bottom, top)
         first_ref[:, columns] = jnp.where(far, across[ROWS:], across[:ROWS])
         second_ref[:, columns] = jnp.where(even, top[:ROWS], bottom[:ROWS])
-    for t in range(tile_rows):
-        inner_ref[:, t * size : (t + 1) * size] = slots[t + REACH][:ROWS]
 
 
 def inner_kernel(
-    field_ref, tiles_ref, mixer_ref, inner_ref, rhs_ref,
+    field_ref, all_tiles_ref, tiles_ref, mixer_ref, masks_ref, rhs_ref,
     main_ref, tiles, rhs, gathered, sems,
 ):
-    terms, tile_rows, _, size, _ = tiles_ref.shape
+    terms, tile_rows, others, size, _ = tiles_ref.shape
     own = field_ref.shape[1]
-    get_tiles = pltpu.make_async_copy(tiles_ref.at[:, :, 0], tiles, sems.at[0])
+    get_tiles = pltpu.make_async_copy(all_tiles_ref.at[:, :, 0], tiles, sems.at[0])
     get_rhs = pltpu.make_async_copy(rhs_ref, rhs, sems.at[1])
     get_tiles.start()
     get_rhs.start()
-    parts = mix(field_ref, mixer_ref, gathered, 1)
+    parts = mix(field_ref, mixer_ref, gathered, 2, 1)
+    wanted = range(REACH, tile_rows + REACH)
+    slots = {t: jnp.zeros((ROWS, size), jnp.float32) for t in wanted}
+    for r in range(tile_rows):
+        product = times_tiles(parts, slice(r * size, (r + 1) * size), beside(tiles_ref, r))
+        add_entries(slots, product, masks_ref, r, others, wanted)
     get_tiles.wait()
     get_rhs.wait()
     for r in range(tile_rows):
         columns = slice(r * size, (r + 1) * size)
         product = times_tiles(parts, columns, tiles[:, r].reshape(terms * size, size))
-        main_ref[:, columns] = rhs[:, columns] - (inner_ref[:, columns] + product)[:own]
+        main_ref[:, columns] = rhs[:, columns] - (slots[r + REACH] + product)[:own]
 
 
 def body(adjoint_field, stiffness_tiles, offsets, galerkin, adjoint_rhs):
@@ -160,7 +176,7 @@
         out_shape=(
             jax.ShapeDtypeStruct((groups, own, dofs), jnp.bfloat16),
             jax.ShapeDtypeStruct((terms, tile_rows, near - 1, size, size), jnp.bfloat16),
-            jax.ShapeDtypeStruct((2, 2 * terms * ROWS, chaos), jnp.bfloat16),
+            jax.ShapeDtypeStruct((2, BLOCKS * terms * ROWS, chaos), jnp.bfloat16),
             jax.ShapeDtypeStruct((n_masks, size), jnp.float32),
         ),
         in_specs=[hbm] * 4,
@@ -169,7 +185,7 @@
             pltpu.VMEM((own, dofs), jnp.bfloat16),
             pltpu.SMEM(offsets.shape, jnp.int32),
             pltpu.VMEM((terms, chaos, chaos), jnp.float32),
-            pltpu.VMEM((2, terms, ROWS, chaos), jnp.float32),
+            pltpu.VMEM((BLOCKS, terms, ROWS, chaos), jnp.float32),
             pltpu.SemaphoreType.DMA((4,)),
         ],
         compiler_params=params,
@@ -178,15 +194,14 @@
     field = lax.all_to_all(copies, "chaos", 0, 0)
 
     halo = REACH * size
-    first, second, inner = pl.pallas_call(
+    first, second = pl.pallas_call(
         halo_kernel,
         out_shape=(
             jax.ShapeDtypeStruct((ROWS, halo), jnp.float32),
             jax.ShapeDtypeStruct((ROWS, halo), jnp.float32),
-            jax.ShapeDtypeStruct((ROWS, dofs), jnp.float32),
         ),
         in_specs=[vmem] * 4,
-        out_specs=(vmem,) * 3,
+        out_specs=(vmem,) * 2,
         scratch_shapes=[pltpu.VMEM((chaos, dofs), jnp.float32)],
         compiler_params=params,
     )(field, tiles, mixer, masks)
@@ -194,7 +209,7 @@
     main = pl.pallas_call(
         inner_kernel,
         out_shape=jax.ShapeDtypeStruct((own, dofs), jnp.float32),
-        in_specs=[vmem, hbm, vmem, vmem, hbm],
+        in_specs=[vmem, hbm, vmem, vmem, vmem, hbm],
         out_specs=vmem,
         scratch_shapes=[
             pltpu.VMEM((terms, tile_rows, size, size), jnp.bfloat16),
@@ -203,10 +218,10 @@
             pltpu.SemaphoreType.DMA((2,)),
         ],
         compiler_params=params,
-    )(field, all_tiles, mixer, inner, rhs)
+    )(field, all_tiles, tiles, mixer, masks, rhs)
 
     def partner(s, c):
-        return (s + 1) * groups + (c ^ turn if s % RUN == RUN - 1 else c)
+        return (s + 1) * groups + (c ^ turn ^ 1 if s % RUN == RUN - 1 else c ^ 1)
 
     pairs = [(s * groups + c, partner(s, c), s) for s in range(slabs - 1) for c in range(groups)]
     axes = ("space", "chaos")

time: 25.6 us -> 25 us (0.977)
  waiting for transfers between devices: 3.56 us -> 2.91 us
  Pallas kernels: 3.71 us -> 4.06 us
  starting transfers between devices: 6.8 us -> 6.52 us
    ppermute x2, waiting for transfers between devices: 3.56 us -> 2.91 us  [swap(): lax.ppermute(x, axes, [p for a, b, s in pairs if s % 2 == parity for p in...]
    pallas_call x1, Pallas kernels: 1.48 us -> 1.83 us  [body(): pl.pallas_call(inner_kernel, out_shape=jax.ShapeDtypeStruct((own, dofs),...]
    ppermute x2, starting transfers between devices: 6.8 us -> 6.52 us  [swap(): lax.ppermute(x, axes, [p for a, b, s in pairs if s % 2 == parity for p in...]
  transfers between devices with their start and end apart: 2 -> 2, of which waited for: 1 -> 1; matrix products, arithmetic and copies ran while one was open for 0% -> 0% of each run, Pallas kernels for 6% -> 7%
where the time goes in v4:
time: 25 us; the launch traced here: 24.8 us
  blocking collectives  10.6 us (42%)
  starting transfers between devices  6.52 us (26%)
  Pallas kernels  4.06 us (16%)
  waiting for transfers between devices  2.91 us (12%)
  other arithmetic  0.62 us (2%)
    all_to_all x1, blocking collectives, body(): field = lax.all_to_all(copies, 'chaos', 0, 0)  10.6 us
    ppermute x2, starting transfers between devices, swap(): lax.ppermute(x, axes, [p for a, b, s in pairs if s % 2 == parity for p in...  6.52 us
    ppermute x2, waiting for transfers between devices, swap(): lax.ppermute(x, axes, [p for a, b, s in pairs if s % 2 == parity for p in...  2.91 us
    pallas_call x1, Pallas kernels, body(): pl.pallas_call(inner_kernel, out_shape=jax.ShapeDtypeStruct((own, dofs),...  1.83 us
    pallas_call x1, Pallas kernels, body(): pl.pallas_call(stage_kernel, out_shape=(jax.ShapeDtypeStruct((groups, own...  1.67 us
    sub x1, other arithmetic, body(): return main - got[:own]  0.61 us
    pallas_call x1, Pallas kernels, body(): pl.pallas_call(halo_kernel, out_shape=(jax.ShapeDtypeStruct((ROWS, halo),...  0.56 us
  transfers between devices with their start and end apart: 2, of which 1 were waited for; matrix products, arithmetic and copies ran while one was open for 0% of the time, Pallas kernels for 7%

profile of v4, /device:TPU:256, one launch (start us, length us, event | category | flops | bytes accessed | tf_op | source)
XLA Modules:
  0.0 24.8 jit_solution(5339040115001376867)
XLA Ops:
  0.0 1.7 %shard_map.55 = (bf16[8,7,512]{2,1,0:T(8,128)(2,1)S(1)}, bf16[7,4,2,128,128]{4,3,2,1,0:T(8,128)(2,1)S(1)}, bf16[2,168,56]{2,1,0:T(8,128)(2,1)S(1)}, f32[64,128]{1,0:T(8,128)S(1)}) custom-call(bf16[7,512]{1,0:T(8,128)(2,1)} %field_ref.1, s32[4,3]{1,0:T(4,128)} %offsets_ref.1, bf16[7,4,3,128,128]{4,3,2,1,0:T(8,128)(2,1)} %all_tiles_ref.1, ...), custom_call_target="tpu_custom_call" | custom-call | tf_op jit(solution)/shard_map/pallas_call | solution.py:174
  1.7 10.6 %all_to_all.5.field_ref = bf16[8,7,512]{2,1,0:T(8,128)(2,1)S(1)} all-to-all(bf16[8,7,512]{2,1,0:T(8,128)(2,1)S(1)} %get-tuple-element.11), channel_id=1, replica_groups=mesh['space'=64,'chaos'=8] {'chaos'}, dimensions={0} | all-to-all | bytes 114688 | tf_op jit(solution)/shard_map/all_to_all | solution.py:194
  12.3 0.6 %shard_map.57 = (f32[8,256]{1,0:T(8,128)S(1)}, f32[8,256]{1,0:T(8,128)S(1)}) custom-call(bf16[8,7,512]{2,1,0:T(8,128)(2,1)S(1)} %all_to_all.5.field_ref, bf16[7,4,2,128,128]{4,3,2,1,0:T(8,128)(2,1)S(1)} %get-tuple-element.12.tiles_ref, bf16[2,168,56]{2,1,0:T(8,128)(2,1)S(1)} %get-tuple-element.13.mixer_ref, f32[64,128]{1,0:T(8,128)S(1)} %get-tuple-element.14.masks_ref), custom_call_target="tpu_custom_call" | custom-call | tf_op jit(solution)/shard_map/pallas_call | solution.py:197
  12.8 4.1 %collective-permute-start = (f32[8,256]{1,0:T(8,128)S(1)}, f32[8,256]{1,0:T(8,128)S(1)}, u32[]{:S(2)}, u32[]{:S(2)}) collective-permute-start(f32[8,256]{1,0:T(8,128)S(1)} %get-tuple-element.15), channel_id=1, source_target_pairs={{8,17},{17,8},{9,16},{16,9},{10,19},{19,10},{11,18},{18,11},{12,21... | collective-permute-start | bytes 24584 | tf_op jit(solution)/shard_map/ppermute | solution.py:230
  17.0 2.4 %collective-permute-start.1 = (f32[8,256]{1,0:T(8,128)S(1)}, f32[8,256]{1,0:T(8,128)S(1)}, u32[]{:S(2)}, u32[]{:S(2)}) collective-permute-start(f32[8,256]{1,0:T(8,128)S(1)} %get-tuple-element.16), channel_id=1, source_target_pairs={{0,9},{9,0},{1,8},{8,1},{2,11},{11,2},{3,10},{10,3},{4,13},{13,4},... | collective-permute-start | bytes 24584 | tf_op jit(solution)/shard_map/ppermute | solution.py:230
  19.4 1.8 %shard_map.56 = f32[7,512]{1,0:T(8,128)S(1)} custom-call(bf16[8,7,512]{2,1,0:T(8,128)(2,1)S(1)} %all_to_all.5.field_ref, bf16[7,4,3,128,128]{4,3,2,1,0:T(8,128)(2,1)} %all_tiles_ref.1, bf16[7,4,2,128,128]{4,3,2,1,0:T(8,128)(2,1)S(1)} %get-tuple-element.12.tiles_ref, bf16[2,168,56]{2,1,0:T(8,128)(2,1)S(1)} %get-tuple-element.13.mixer_ref, ...), custom_call_target="tpu_custom_call" | custom-call | tf_op jit(solution)/shard_map/pallas_call | solution.py:209
  21.2 2.9 %collective-permute-done = f32[8,256]{1,0:T(8,128)S(1)} collective-permute-done((f32[8,256]{1,0:T(8,128)S(1)}, f32[8,256]{1,0:T(8,128)S(1)}, u32[]{:S(2)}, u32[]{:S(2)}) %collective-permute-start) | collective-permute-done | bytes 8224 | tf_op jit(solution)/shard_map/ppermute | solution.py:230
  24.1 0.0 collective-permute-done.1
  24.1 0.6 %fusion = f32[7,512]{1,0:T(8,128)} fusion(f32[7,512]{1,0:T(8,128)S(1)} %shard_map.56, f32[8,256]{1,0:T(8,128)S(1)} %get-tuple-element.18, f32[8,256]{1,0:T(8,128)S(1)} %get-tuple-element.17), kind=kLoop, calls=%fused_computation.1 | loop fusion | flops 7168 | bytes 45056 | tf_op jit(solution)/shard_map/sub | solution.py:237
  (1 shorter events, 0.0 us)
Async XLA Ops:
  12.8 11.3 %collective-permute-start = (f32[8,256]{1,0:T(8,128)S(1)}, f32[8,256]{1,0:T(8,128)S(1)}, u32[]{:S(2)}, u32[]{:S(2)}) collective-permute-start(f32[8,256]{1,0:T(8,128)S(1)} %get-tuple-element.15), channel_id=1, source_target_pairs={{8,17},{17,8},{9,16},{16,9},{10,19},{19,10},{11,18},{18,11},{12,21... | collective-permute-start | bytes 24584 | tf_op jit(solution)/shard_map/ppermute | solution.py:230
  17.0 7.2 %collective-permute-start.1 = (f32[8,256]{1,0:T(8,128)S(1)}, f32[8,256]{1,0:T(8,128)S(1)}, u32[]{:S(2)}, u32[]{:S(2)}) collective-permute-start(f32[8,256]{1,0:T(8,128)S(1)} %get-tuple-element.16), channel_id=1, source_target_pairs={{0,9},{9,0},{1,8},{8,1},{2,11},{11,2},{3,10},{10,3},{4,13},{13,4},... | collective-permute-start | bytes 24584 | tf_op jit(solution)/shard_map/ppermute | solution.py:230

commit v5 on v3

v5 whole, which is shorter than its diff:
```python
import functools

import jax
import jax.numpy as jnp
from jax import lax
from jax.experimental import pallas as pl
from jax.experimental.pallas import tpu as pltpu
from jax.sharding import PartitionSpec as P

ROWS = 8
REACH = 2
SPAN = 2 * REACH + 1
RUN = 4
BLOCKS = 3


def in_hbm(x):
    return pltpu.with_memory_space_constraint(x, pltpu.HBM)


def split(x):
    high = x.astype(jnp.bfloat16).astype(jnp.float32)
    return high, x - high


def stage_kernel(
    field_ref, offsets_ref, tiles_ref, galerkin_ref,
    copies_out, first_tiles, second_tiles, mixer_out, first_masks, second_masks, own_masks,
    field, offsets, galerkin, mixer, sems,
):
    terms, tile_rows, near, _, _ = tiles_ref.shape
    groups, own, _ = copies_out.shape
    space, block = lax.axis_index("space"), lax.axis_index("chaos")
    odd = lax.rem(space, 2)
    first_row = odd * (tile_rows - REACH)
    second_row = (1 - odd) * (tile_rows - REACH)
    pairs = [(field_ref, field), (galerkin_ref, galerkin), (offsets_ref, offsets)]
    for row, out in ((first_row, first_tiles), (second_row, second_tiles)):
        pairs.append((tiles_ref.at[:, pl.ds(row, REACH), 1:near], out))
    moves = [pltpu.make_async_copy(a, b, sems.at[i]) for i, (a, b) in enumerate(pairs)]
    for move in moves:
        move.start()
    moves[0].wait()
    value = field[...]
    for g in range(groups):
        copies_out[g] = value
    mixer[...] = jnp.zeros_like(mixer)
    moves[1].wait()
    half = groups // 2
    crossed = block + 1 - 2 * lax.rem(block, 2)
    far_off = jnp.where(crossed < half, crossed + half, crossed - half)
    place = lax.rem(space, RUN)
    at_end = jnp.logical_or(place == 0, place == RUN - 1)
    for b, owner in enumerate((jnp.where(at_end, far_off, block), block, block)):
        for k in range(terms):
            mixer[b, k, :own, :] = galerkin[k, pl.ds(owner * own, own), :]
    parts = split(mixer[...].reshape(BLOCKS, terms * ROWS, groups * own))
    mixer_out[...] = jnp.concatenate(parts, axis=1).astype(jnp.bfloat16)
    moves[2].wait()

    def row_of(flag):
        return jnp.full((1, own_masks.shape[1]), flag.astype(jnp.float32))

    for row, out in ((first_row, first_masks), (second_row, second_masks)):
        below = jnp.where(row == 0, -REACH, tile_rows)
        for i in range(REACH):
            for s in range(1, near):
                for t in range(REACH):
                    at = (i * (near - 1) + s - 1) * REACH + t
                    out[at : at + 1, :] = row_of(row + i + offsets[row + i, s] == below + t)
    for r in range(tile_rows):
        for s in range(1, near):
            for t in range(tile_rows):
                at = (r * (near - 1) + s - 1) * tile_rows + t
                own_masks[at : at + 1, :] = row_of(r + offsets[r, s] == t)
    for move in moves[3:]:
        move.wait()


def mix(field_ref, mixer_ref, block, columns, gathered):
    groups, own, _ = field_ref.shape
    rows = mixer_ref.shape[1] // 2
    for g in range(groups):
        gathered[g * own : (g + 1) * own, :] = field_ref[g, :, columns].astype(jnp.float32)
    field = gathered[...].astype(jnp.bfloat16)
    both = jnp.dot(mixer_ref[block], field, preferred_element_type=jnp.float32)
    mixed = (both[:rows] + both[rows:]).reshape(rows // ROWS, ROWS, field.shape[1])
    return split(mixed)


def times_tiles(parts, columns, tiles):
    terms, near, size, _ = tiles.shape
    left = jnp.concatenate(
        [jnp.concatenate([part[k, :, columns] for part in parts], axis=0) for k in range(terms)],
        axis=1,
    ).astype(jnp.bfloat16)
    right = jnp.concatenate([tiles[:, s].reshape(terms * size, size) for s in range(near)], axis=1)
    product = jnp.dot(left, right, preferred_element_type=jnp.float32)
    product = product[:ROWS] + product[ROWS:]
    return [product[:, s * size : (s + 1) * size] for s in range(near)]


def halo_kernel(which, field_ref, tiles_ref, mixer_ref, masks_ref, halo_ref, gathered):
    others, size = tiles_ref.shape[2:4]
    tile_rows = field_ref.shape[2] // size
    odd = lax.rem(lax.axis_index("space"), 2)
    row = (odd if which == 0 else 1 - odd) * (tile_rows - REACH)
    columns = pl.ds(pl.multiple_of(row * size, size), REACH * size)
    parts = mix(field_ref, mixer_ref, which, columns, gathered)
    halos = [jnp.zeros((ROWS, size), jnp.float32) for _ in range(REACH)]
    for i in range(REACH):
        entries = times_tiles(parts, slice(i * size, (i + 1) * size), tiles_ref[:, i])
        for s in range(others):
            for t in range(REACH):
                at = (i * others + s) * REACH + t
                halos[t] += jnp.where(masks_ref[at : at + 1, :] > 0, entries[s], 0.0)
    for t in range(REACH):
        halo_ref[:, t * size : (t + 1) * size] = halos[t]


def own_kernel(
    field_ref, tiles_hbm, mixer_ref, masks_ref, rhs_hbm,
    main_ref, tiles, rhs, gathered, sems,
):
    _, tile_rows, near, size, _ = tiles.shape
    own = field_ref.shape[1]
    get_rhs = pltpu.make_async_copy(rhs_hbm, rhs, sems.at[0])
    get_tiles = [
        pltpu.make_async_copy(tiles_hbm.at[:, r], tiles.at[:, r], sems.at[1 + r])
        for r in range(tile_rows)
    ]
    for move in (*get_tiles, get_rhs):
        move.start()
    parts = mix(field_ref, mixer_ref, BLOCKS - 1, slice(None), gathered)
    sums = [jnp.zeros((ROWS, size), jnp.float32) for _ in range(tile_rows)]
    for r in range(tile_rows):
        get_tiles[r].wait()
        entries = times_tiles(parts, slice(r * size, (r + 1) * size), tiles[:, r])
        sums[r] += entries[0]
        for s in range(1, near):
            for t in range(tile_rows):
                if abs(t - r) > REACH or t == r:
                    continue
                at = (r * (near - 1) + s - 1) * tile_rows + t
                sums[t] += jnp.where(masks_ref[at : at + 1, :] > 0, entries[s], 0.0)
    get_rhs.wait()
    for t in range(tile_rows):
        columns = slice(t * size, (t + 1) * size)
        main_ref[:, columns] = rhs[:, columns] - sums[t][:own]


def body(adjoint_field, stiffness_tiles, offsets, galerkin, adjoint_rhs):
    terms, tile_rows, near, size, _ = stiffness_tiles.shape
    own, dofs = adjoint_field.shape
    groups, slabs = lax.axis_size("chaos"), lax.axis_size("space")
    chaos = own * groups
    turn = groups // 2
    vmem = pl.BlockSpec(memory_space=pltpu.VMEM)
    hbm = pl.BlockSpec(memory_space=pltpu.HBM)
    params = pltpu.CompilerParams(vmem_limit_bytes=24 * 1024 * 1024)
    all_tiles, rhs = in_hbm(stiffness_tiles), in_hbm(adjoint_rhs)

    def floats(*shape):
        return jax.ShapeDtypeStruct(shape, jnp.float32)

    def halves(*shape):
        return jax.ShapeDtypeStruct(shape, jnp.bfloat16)

    side = (terms, REACH, near - 1, size, size)
    side_masks = REACH * (near - 1) * REACH
    copies, first_tiles, second_tiles, mixer, first_masks, second_masks, own_masks = pl.pallas_call(
        stage_kernel,
        out_shape=(
            halves(groups, own, dofs),
            halves(*side),
            halves(*side),
            halves(BLOCKS, 2 * terms * ROWS, chaos),
            floats(side_masks, size),
            floats(side_masks, size),
            floats(tile_rows * (near - 1) * tile_rows, size),
        ),
        in_specs=[hbm] * 4,
        out_specs=(vmem,) * 7,
        scratch_shapes=[
            pltpu.VMEM((own, dofs), jnp.bfloat16),
            pltpu.SMEM(offsets.shape, jnp.int32),
            pltpu.VMEM((terms, chaos, chaos), jnp.float32),
            pltpu.VMEM((BLOCKS, terms, ROWS, chaos), jnp.float32),
            pltpu.SemaphoreType.DMA((5,)),
        ],
        compiler_params=params,
    )(in_hbm(adjoint_field), in_hbm(offsets), all_tiles, in_hbm(galerkin))

    field = lax.all_to_all(copies, "chaos", 0, 0)

    def halo_of(which, tiles, masks):
        return pl.pallas_call(
            functools.partial(halo_kernel, which),
            out_shape=floats(ROWS, REACH * size),
            in_specs=[vmem] * 4,
            out_specs=vmem,
            scratch_shapes=[pltpu.VMEM((chaos, REACH * size), jnp.float32)],
            compiler_params=params,
        )(field, tiles, mixer, masks)

    first = halo_of(0, first_tiles, first_masks)
    second = halo_of(1, second_tiles, second_masks)

    main = pl.pallas_call(
        own_kernel,
        out_shape=floats(own, dofs),
        in_specs=[vmem, hbm, vmem, vmem, hbm],
        out_specs=vmem,
        scratch_shapes=[
            pltpu.VMEM(stiffness_tiles.shape, jnp.bfloat16),
            pltpu.VMEM((own, dofs), jnp.float32),
            pltpu.VMEM((chaos, dofs), jnp.float32),
            pltpu.SemaphoreType.DMA((1 + tile_rows,)),
        ],
        compiler_params=params,
    )(field, all_tiles, mixer, own_masks, rhs)

    def partner(s, c):
        return (s + 1) * groups + (c ^ turn ^ 1 if s % RUN == RUN - 1 else c)

    pairs = [(s * groups + c, partner(s, c), s) for s in range(slabs - 1) for c in range(groups)]
    axes = ("space", "chaos")

    def swap(x, parity):
        return lax.ppermute(x, axes, [p for a, b, s in pairs if s % 2 == parity for p in ((a, b), (b, a))])

    got_first, got_second = swap(first, 1), swap(second, 0)
    even = (lax.axis_index("space") % 2) == 0
    halo_a = jnp.where(even, got_first, got_second)
    halo_b = jnp.where(even, got_second, got_first)
    got = jnp.concatenate([halo_a, halo_b], axis=1)
    return main - got[:own]


def solution(mesh):
    return jax.shard_map(
        body,
        mesh=mesh,
        in_specs=(
            P("chaos", "space"),
            P(None, "space", None, None, None),
            P("space", None),
            P(),
            P("chaos", "space"),
        ),
        out_specs=P("chaos", "space"),
        check_vma=False,
    )
```

time: 25.6 us -> 24.8 us (0.969)
  waiting for transfers between devices: 3.56 us -> 1.98 us
  Pallas kernels: 3.71 us -> 4.49 us
    ppermute x2, waiting for transfers between devices: 3.56 us -> 1.98 us  [swap(): lax.ppermute(x, axes, [p for a, b, s in pairs if s % 2 == parity for p in...]
    pallas_call x3 -> x4, Pallas kernels: 3.71 us -> 4.49 us  [the longest x1 2.12 us: body(): pl.pallas_call(own_kernel, out_shape=floats(own, dofs), in_specs=[vmem, h...]
  transfers between devices with their start and end apart: 2 -> 2, of which waited for: 1 -> 1; matrix products, arithmetic and copies ran while one was open for 0% -> 0% of each run, Pallas kernels for 6% -> 10%
where the time goes in v5:
time: 24.8 us; the launch traced here: 24.5 us
  blocking collectives  10.6 us (43%)
  starting transfers between devices  6.79 us (27%)
  Pallas kernels  4.49 us (18%)
  waiting for transfers between devices  1.98 us (8%)
  other arithmetic  0.62 us (2%)
    all_to_all x1, blocking collectives, body(): field = lax.all_to_all(copies, 'chaos', 0, 0)  10.6 us
    ppermute x2, starting transfers between devices, swap(): lax.ppermute(x, axes, [p for a, b, s in pairs if s % 2 == parity for p in...  6.79 us
    pallas_call x1, Pallas kernels, body(): pl.pallas_call(own_kernel, out_shape=floats(own, dofs), in_specs=[vmem, h...  2.12 us
    ppermute x2, waiting for transfers between devices, swap(): lax.ppermute(x, axes, [p for a, b, s in pairs if s % 2 == parity for p in...  1.98 us
    pallas_call x1, Pallas kernels, body(): pl.pallas_call(stage_kernel, out_shape=(halves(groups, own, dofs), halves...  1.63 us
    pallas_call x2, Pallas kernels, halo_of(): pl.pallas_call(functools.partial(halo_kernel, which), out_shape=floats(RO...  0.75 us
    sub x1, other arithmetic, body(): return main - got[:own]  0.61 us
  transfers between devices with their start and end apart: 2, of which 1 were waited for; matrix products, arithmetic and copies ran while one was open for 0% of the time, Pallas kernels for 10%

profile of v5, /device:TPU:256, one launch (start us, length us, event | category | flops | bytes accessed | tf_op | source)
XLA Modules:
  0.0 24.5 jit_solution(13683401194318448008)
XLA Ops:
  0.0 1.6 %shard_map.55 = (bf16[8,7,512]{2,1,0:T(8,128)(2,1)S(1)}, bf16[7,2,2,128,128]{4,3,2,1,0:T(8,128)(2,1)S(1)}, bf16[7,2,2,128,128]{4,3,2,1,0:T(8,128)(2,1)S(1)}, bf1...) custom-call(bf16[7,512]{1,0:T(8,128)(2,1)} %field_ref.1, ...), custom_call_target="tpu_custom_call" | custom-call | tf_op jit(solution)/shard_map/pallas_call | solution.py:171
  1.6 10.6 %all_to_all.5.field_ref = bf16[8,7,512]{2,1,0:T(8,128)(2,1)S(1)} all-to-all(bf16[8,7,512]{2,1,0:T(8,128)(2,1)S(1)} %get-tuple-element.12), channel_id=1, replica_groups=mesh['space'=64,'chaos'=8] {'chaos'}, dimensions={0} | all-to-all | bytes 114688 | tf_op jit(solution)/shard_map/all_to_all | solution.py:194
  12.2 0.4 %shard_map.57 = f32[8,256]{1,0:T(8,128)S(1)} custom-call(bf16[8,7,512]{2,1,0:T(8,128)(2,1)S(1)} %all_to_all.5.field_ref, bf16[7,2,2,128,128]{4,3,2,1,0:T(8,128)(2,1)S(1)} %get-tuple-element.15.tiles_ref, bf16[3,112,56]{2,1,0:T(8,128)(2,1)S(1)} %get-tuple-element.13.mixer_ref, f32[8,128]{1,0:T(8,128)S(1)} %get-tuple-element.16.masks_ref), custom_call_target="tpu_custom_call" | custom-call | tf_op jit(solution)/shard_map/pallas_call | solution.py:197
  12.6 4.1 %collective-permute-start = (f32[8,256]{1,0:T(8,128)S(1)}, f32[8,256]{1,0:T(8,128)S(1)}, u32[]{:S(2)}, u32[]{:S(2)}) collective-permute-start(f32[8,256]{1,0:T(8,128)S(1)} %shard_map.57), channel_id=1, source_target_pairs={{8,16},{16,8},{9,17},{17,9},{10,18},{18,10},{11,19},{19,11},{12,20... | collective-permute-start | bytes 24584 | tf_op jit(solution)/shard_map/ppermute | solution.py:230
  16.7 0.4 %shard_map.58 = f32[8,256]{1,0:T(8,128)S(1)} custom-call(bf16[8,7,512]{2,1,0:T(8,128)(2,1)S(1)} %all_to_all.5.field_ref, bf16[7,2,2,128,128]{4,3,2,1,0:T(8,128)(2,1)S(1)} %get-tuple-element.17.tiles_ref, bf16[3,112,56]{2,1,0:T(8,128)(2,1)S(1)} %get-tuple-element.13.mixer_ref, f32[8,128]{1,0:T(8,128)S(1)} %get-tuple-element.18.masks_ref), custom_call_target="tpu_custom_call" | custom-call | tf_op jit(solution)/shard_map/pallas_call | solution.py:197
  17.1 2.7 %collective-permute-start.1 = (f32[8,256]{1,0:T(8,128)S(1)}, f32[8,256]{1,0:T(8,128)S(1)}, u32[]{:S(2)}, u32[]{:S(2)}) collective-permute-start(f32[8,256]{1,0:T(8,128)S(1)} %shard_map.58), channel_id=1, source_target_pairs={{0,8},{8,0},{1,9},{9,1},{2,10},{10,2},{3,11},{11,3},{4,12},{12,4},... | collective-permute-start | bytes 24584 | tf_op jit(solution)/shard_map/ppermute | solution.py:230
  19.8 2.1 %shard_map.56 = f32[7,512]{1,0:T(8,128)S(1)} custom-call(bf16[8,7,512]{2,1,0:T(8,128)(2,1)S(1)} %all_to_all.5.field_ref, bf16[7,4,3,128,128]{4,3,2,1,0:T(8,128)(2,1)} %tiles_hbm.1, bf16[3,112,56]{2,1,0:T(8,128)(2,1)S(1)} %get-tuple-element.13.mixer_ref, f32[32,128]{1,0:T(8,128)S(1)} %get-tuple-element.14.masks_ref, f32[7,512]{1,0:T(8,128)} %rhs_hbm.1), custom_call_target="tpu_custom_call" | custom-call | tf_op jit(solution)/shard_map/pallas_call | solution.py:209
  21.9 2.0 %collective-permute-done = f32[8,256]{1,0:T(8,128)S(1)} collective-permute-done((f32[8,256]{1,0:T(8,128)S(1)}, f32[8,256]{1,0:T(8,128)S(1)}, u32[]{:S(2)}, u32[]{:S(2)}) %collective-permute-start) | collective-permute-done | bytes 8224 | tf_op jit(solution)/shard_map/ppermute | solution.py:230
  23.9 0.0 collective-permute-done.1
  23.9 0.6 %fusion = f32[7,512]{1,0:T(8,128)} fusion(f32[7,512]{1,0:T(8,128)S(1)} %shard_map.56, f32[8,256]{1,0:T(8,128)S(1)} %get-tuple-element.20, f32[8,256]{1,0:T(8,128)S(1)} %get-tuple-element.19), kind=kLoop, calls=%fused_computation.1 | loop fusion | flops 7168 | bytes 45056 | tf_op jit(solution)/shard_map/sub | solution.py:237
  (1 shorter events, 0.0 us)
Async XLA Ops:
  12.6 11.3 %collective-permute-start = (f32[8,256]{1,0:T(8,128)S(1)}, f32[8,256]{1,0:T(8,128)S(1)}, u32[]{:S(2)}, u32[]{:S(2)}) collective-permute-start(f32[8,256]{1,0:T(8,128)S(1)} %shard_map.57), channel_id=1, source_target_pairs={{8,16},{16,8},{9,17},{17,9},{10,18},{18,10},{11,19},{19,11},{12,20... | collective-permute-start | bytes 24584 | tf_op jit(solution)/shard_map/ppermute | solution.py:230
  17.1 6.8 %collective-permute-start.1 = (f32[8,256]{1,0:T(8,128)S(1)}, f32[8,256]{1,0:T(8,128)S(1)}, u32[]{:S(2)}, u32[]{:S(2)}) collective-permute-start(f32[8,256]{1,0:T(8,128)S(1)} %shard_map.58), channel_id=1, source_target_pairs={{0,8},{8,0},{1,9},{9,1},{2,10},{10,2},{3,11},{11,3},{4,12},{12,4},... | collective-permute-start | bytes 24584 | tf_op jit(solution)/shard_map/ppermute | solution.py:230

commit v6 on v5

--- a/solution.py
+++ b/solution.py
@@ -1,5 +1,3 @@
-import functools
-
 import jax
 import jax.numpy as jnp
 from jax import lax
@@ -11,7 +9,17 @@
 REACH = 2
 SPAN = 2 * REACH + 1
 RUN = 4
+ACROSS = (3, 2, 0, 1)
 BLOCKS = 3
+
+
+def across(c):
+    return 2 * ACROSS[c // 2] + 1 - c % 2
+
+
+def is_late():
+    upper = lax.rem(lax.axis_index("space") // RUN, 2)
+    return lax.axis_index("chaos") // 2 == (1 - upper) * (lax.axis_size("chaos") // 2 - 1)
 
 
 def in_hbm(x):
@@ -23,40 +31,46 @@
     return high, x - high
 
 
-def stage_kernel(
-    field_ref, offsets_ref, tiles_ref, galerkin_ref,
-    copies_out, first_tiles, second_tiles, mixer_out, first_masks, second_masks, own_masks,
-    field, offsets, galerkin, mixer, sems,
-):
-    terms, tile_rows, near, _, _ = tiles_ref.shape
-    groups, own, _ = copies_out.shape
+def moves_of(hbm_refs, staged, scratch, first=0, last=4):
+    offsets_hbm, tiles_hbm, galerkin_hbm = hbm_refs
+    offsets, galerkin, _, sems = scratch
+    tile_rows, near = tiles_hbm.shape[1:3]
+    first_row, second_row = side_rows(tile_rows)
+    pairs = [(galerkin_hbm, galerkin), (offsets_hbm, offsets)]
+    for row, out in zip((first_row, second_row), staged[:2]):
+        pairs.append((tiles_hbm.at[:, pl.ds(row, REACH), 1:near], out))
+    return [pltpu.make_async_copy(*pairs[i], sems.at[i]) for i in range(first, last)]
+
+
+def side_rows(tile_rows):
+    odd = lax.rem(lax.axis_index("space"), 2)
+    return odd * (tile_rows - REACH), (1 - odd) * (tile_rows - REACH)
+
+
+def stage(hbm_refs, staged, scratch):
+    _, _, mixer_out, first_masks, second_masks, own_masks = staged
+    offsets, galerkin, mixer, _ = scratch
+    moves = moves_of(hbm_refs, staged, scratch, 0, 2)
+    terms, tile_rows, near, _, _ = hbm_refs[1].shape
+    groups = lax.axis_size("chaos")
+    own = galerkin.shape[1] // groups
     space, block = lax.axis_index("space"), lax.axis_index("chaos")
-    odd = lax.rem(space, 2)
-    first_row = odd * (tile_rows - REACH)
-    second_row = (1 - odd) * (tile_rows - REACH)
-    pairs = [(field_ref, field), (galerkin_ref, galerkin), (offsets_ref, offsets)]
-    for row, out in ((first_row, first_tiles), (second_row, second_tiles)):
-        pairs.append((tiles_ref.at[:, pl.ds(row, REACH), 1:near], out))
-    moves = [pltpu.make_async_copy(a, b, sems.at[i]) for i, (a, b) in enumerate(pairs)]
-    for move in moves:
-        move.start()
+    mixer[...] = jnp.zeros_like(mixer)
     moves[0].wait()
-    value = field[...]
-    for g in range(groups):
-        copies_out[g] = value
-    mixer[...] = jnp.zeros_like(mixer)
-    moves[1].wait()
-    half = groups // 2
-    crossed = block + 1 - 2 * lax.rem(block, 2)
-    far_off = jnp.where(crossed < half, crossed + half, crossed - half)
     place = lax.rem(space, RUN)
     at_end = jnp.logical_or(place == 0, place == RUN - 1)
+    far_off = block
+    for c in range(groups):
+        here = jnp.where(place == 0, across(c) == block, c == block)
+        far_off = jnp.where(here, jnp.where(place == 0, c, across(c)), far_off)
     for b, owner in enumerate((jnp.where(at_end, far_off, block), block, block)):
         for k in range(terms):
             mixer[b, k, :own, :] = galerkin[k, pl.ds(owner * own, own), :]
     parts = split(mixer[...].reshape(BLOCKS, terms * ROWS, groups * own))
     mixer_out[...] = jnp.concatenate(parts, axis=1).astype(jnp.bfloat16)
-    moves[2].wait()
+    moves[1].wait()
+
+    first_row, second_row = side_rows(tile_rows)
 
     def row_of(flag):
         return jnp.full((1, own_masks.shape[1]), flag.astype(jnp.float32))
@@ -73,8 +87,34 @@
             for t in range(tile_rows):
                 at = (r * (near - 1) + s - 1) * tile_rows + t
                 own_masks[at : at + 1, :] = row_of(r + offsets[r, s] == t)
-    for move in moves[3:]:
-        move.wait()
+
+
+def stage_kernel(
+    field_ref, offsets_hbm, tiles_hbm, galerkin_hbm,
+    copies_out, first_tiles, second_tiles, mixer_out, first_masks, second_masks, own_masks,
+    offsets, galerkin, mixer, sems, field, field_sem,
+):
+    hbm_refs = offsets_hbm, tiles_hbm, galerkin_hbm
+    staged = first_tiles, second_tiles, mixer_out, first_masks, second_masks, own_masks
+    scratch = offsets, galerkin, mixer, sems
+    get_field = pltpu.make_async_copy(field_ref, field, field_sem)
+    get_field.start()
+
+    @pl.when(jnp.logical_not(is_late()))
+    def _():
+        for move in moves_of(hbm_refs, staged, scratch):
+            move.start()
+
+    get_field.wait()
+    value = field[...]
+    for g in range(copies_out.shape[0]):
+        copies_out[g] = value
+
+    @pl.when(jnp.logical_not(is_late()))
+    def _():
+        stage(hbm_refs, staged, scratch)
+        for move in moves_of(hbm_refs, staged, scratch, 2):
+            move.wait()
 
 
 def mix(field_ref, mixer_ref, block, columns, gathered):
@@ -100,13 +140,14 @@
     return [product[:, s * size : (s + 1) * size] for s in range(near)]
 
 
-def halo_kernel(which, field_ref, tiles_ref, mixer_ref, masks_ref, halo_ref, gathered):
+def side_parts(which, field_ref, mixer_ref, size, gathered):
+    row = side_rows(field_ref.shape[2] // size)[which]
+    columns = pl.ds(pl.multiple_of(row * size, size), REACH * size)
+    return mix(field_ref, mixer_ref, which, columns, gathered)
+
+
+def side_halo(parts, tiles_ref, masks_ref, halo_ref):
     others, size = tiles_ref.shape[2:4]
-    tile_rows = field_ref.shape[2] // size
-    odd = lax.rem(lax.axis_index("space"), 2)
-    row = (odd if which == 0 else 1 - odd) * (tile_rows - REACH)
-    columns = pl.ds(pl.multiple_of(row * size, size), REACH * size)
-    parts = mix(field_ref, mixer_ref, which, columns, gathered)
     halos = [jnp.zeros((ROWS, size), jnp.float32) for _ in range(REACH)]
     for i in range(REACH):
         entries = times_tiles(parts, slice(i * size, (i + 1) * size), tiles_ref[:, i])
@@ -116,6 +157,28 @@
                 halos[t] += jnp.where(masks_ref[at : at + 1, :] > 0, entries[s], 0.0)
     for t in range(REACH):
         halo_ref[:, t * size : (t + 1) * size] = halos[t]
+
+
+def halos_kernel(*refs):
+    field_ref, hbm_refs, halo_refs = refs[0], refs[7:10], refs[10:12]
+    staged, scratch, gathered = refs[12:18], refs[18:22], refs[22]
+
+    @pl.when(is_late())
+    def _():
+        for move in moves_of(hbm_refs, staged, scratch):
+            move.start()
+        stage(hbm_refs, staged, scratch)
+
+    size = staged[0].shape[3]
+    parts = [side_parts(which, field_ref, staged[2], size, gathered.at[which]) for which in range(2)]
+
+    @pl.when(is_late())
+    def _():
+        for move in moves_of(hbm_refs, staged, scratch, 2):
+            move.wait()
+
+    for which in range(2):
+        side_halo(parts[which], staged[which], staged[3 + which], halo_refs[which])
 
 
 def own_kernel(
@@ -154,7 +217,6 @@
     own, dofs = adjoint_field.shape
     groups, slabs = lax.axis_size("chaos"), lax.axis_size("space")
     chaos = own * groups
-    turn = groups // 2
     vmem = pl.BlockSpec(memory_space=pltpu.VMEM)
     hbm = pl.BlockSpec(memory_space=pltpu.HBM)
     params = pltpu.CompilerParams(vmem_limit_bytes=24 * 1024 * 1024)
@@ -168,43 +230,43 @@
 
     side = (terms, REACH, near - 1, size, size)
     side_masks = REACH * (near - 1) * REACH
-    copies, first_tiles, second_tiles, mixer, first_masks, second_masks, own_masks = pl.pallas_call(
+    staged_shapes = (
+        halves(*side),
+        halves(*side),
+        halves(BLOCKS, 2 * terms * ROWS, chaos),
+        floats(side_masks, size),
+        floats(side_masks, size),
+        floats(tile_rows * (near - 1) * tile_rows, size),
+    )
+    stage_scratch = [
+        pltpu.SMEM(offsets.shape, jnp.int32),
+        pltpu.VMEM((terms, chaos, chaos), jnp.float32),
+        pltpu.VMEM((BLOCKS, terms, ROWS, chaos), jnp.float32),
+        pltpu.SemaphoreType.DMA((4,)),
+    ]
+    sources = in_hbm(offsets), all_tiles, in_hbm(galerkin)
+    copies, *staged = pl.pallas_call(
         stage_kernel,
-        out_shape=(
-            halves(groups, own, dofs),
-            halves(*side),
-            halves(*side),
-            halves(BLOCKS, 2 * terms * ROWS, chaos),
-            floats(side_masks, size),
-            floats(side_masks, size),
-            floats(tile_rows * (near - 1) * tile_rows, size),
-        ),
+        out_shape=(halves(groups, own, dofs), *staged_shapes),
         in_specs=[hbm] * 4,
         out_specs=(vmem,) * 7,
-        scratch_shapes=[
-            pltpu.VMEM((own, dofs), jnp.bfloat16),
-            pltpu.SMEM(offsets.shape, jnp.int32),
-            pltpu.VMEM((terms, chaos, chaos), jnp.float32),
-            pltpu.VMEM((BLOCKS, terms, ROWS, chaos), jnp.float32),
-            pltpu.SemaphoreType.DMA((5,)),
-        ],
+        scratch_shapes=[*stage_scratch, pltpu.VMEM((own, dofs), jnp.bfloat16), pltpu.SemaphoreType.DMA],
         compiler_params=params,
-    )(in_hbm(adjoint_field), in_hbm(offsets), all_tiles, in_hbm(galerkin))
+    )(in_hbm(adjoint_field), *sources)
 
     field = lax.all_to_all(copies, "chaos", 0, 0)
 
-    def halo_of(which, tiles, masks):
-        return pl.pallas_call(
-            functools.partial(halo_kernel, which),
-            out_shape=floats(ROWS, REACH * size),
-            in_specs=[vmem] * 4,
-            out_specs=vmem,
-            scratch_shapes=[pltpu.VMEM((chaos, REACH * size), jnp.float32)],
-            compiler_params=params,
-        )(field, tiles, mixer, masks)
-
-    first = halo_of(0, first_tiles, first_masks)
-    second = halo_of(1, second_tiles, second_masks)
+    halo = floats(ROWS, REACH * size)
+    first, second, *staged = pl.pallas_call(
+        halos_kernel,
+        out_shape=(halo, halo, *staged_shapes),
+        in_specs=[vmem] * 7 + [hbm] * 3,
+        out_specs=(vmem,) * 8,
+        input_output_aliases={1 + i: 2 + i for i in range(6)},
+        scratch_shapes=[*stage_scratch, pltpu.VMEM((2, chaos, REACH * size), jnp.float32)],
+        compiler_params=params,
+    )(field, *staged, *sources)
+    mixer, own_masks = staged[2], staged[5]
 
     main = pl.pallas_call(
         own_kernel,
@@ -221,7 +283,7 @@
     )(field, all_tiles, mixer, own_masks, rhs)
 
     def partner(s, c):
-        return (s + 1) * groups + (c ^ turn ^ 1 if s % RUN == RUN - 1 else c)
+        return (s + 1) * groups + (across(c) if s % RUN == RUN - 1 else c)
 
     pairs = [(s * groups + c, partner(s, c), s) for s in range(slabs - 1) for c in range(groups)]
     axes = ("space", "chaos")

time: 24.8 us -> 24.1 us (0.972)
  blocking collectives: 10.6 us -> 9.71 us
  waiting for transfers between devices: 1.98 us -> 2.35 us
    all_to_all x1, blocking collectives: 10.6 us -> 9.71 us  [body(): field = lax.all_to_all(copies, 'chaos', 0, 0)]
    ppermute x2, waiting for transfers between devices: 1.98 us -> 2.35 us  [swap(): lax.ppermute(x, axes, [p for a, b, s in pairs if s % 2 == parity for p in...]
    pallas_call x3 -> x2, Pallas kernels: 2.37 us -> 2.21 us  [the longest x1 1.63 us: body(): pl.pallas_call(stage_kernel, out_shape=(halves(groups, own, dofs), *stage...]
  transfers between devices with their start and end apart: 2 -> 2, of which waited for: 1 -> 1; matrix products, arithmetic and copies ran while one was open for 0% -> 0% of each run, Pallas kernels for 10% -> 9%
where the time goes in v6:
time: 24.1 us; the launch traced here: 23.9 us
  blocking collectives  9.71 us (40%)
  starting transfers between devices  6.8 us (28%)
  Pallas kernels  4.32 us (18%)
  waiting for transfers between devices  2.35 us (10%)
  other arithmetic  0.62 us (3%)
    all_to_all x1, blocking collectives, body(): field = lax.all_to_all(copies, 'chaos', 0, 0)  9.71 us
    ppermute x2, starting transfers between devices, swap(): lax.ppermute(x, axes, [p for a, b, s in pairs if s % 2 == parity for p in...  6.8 us
    ppermute x2, waiting for transfers between devices, swap(): lax.ppermute(x, axes, [p for a, b, s in pairs if s % 2 == parity for p in...  2.35 us
    pallas_call x1, Pallas kernels, body(): pl.pallas_call(own_kernel, out_shape=floats(own, dofs), in_specs=[vmem, h...  2.12 us
    pallas_call x1, Pallas kernels, body(): pl.pallas_call(stage_kernel, out_shape=(halves(groups, own, dofs), *stage...  1.63 us
    sub x1, other arithmetic, body(): return main - got[:own]  0.61 us
    pallas_call x1, Pallas kernels, body(): pl.pallas_call(halos_kernel, out_shape=(halo, halo, *staged_shapes), in_s...  0.58 us
  transfers between devices with their start and end apart: 2, of which 1 were waited for; matrix products, arithmetic and copies ran while one was open for 0% of the time, Pallas kernels for 9%

profile of v6, /device:TPU:256, one launch (start us, length us, event | category | flops | bytes accessed | tf_op | source)
XLA Modules:
  0.0 23.9 jit_solution(11637414168738200722)
XLA Ops:
  0.0 1.6 %shard_map.55 = (bf16[8,7,512]{2,1,0:T(8,128)(2,1)S(1)}, bf16[7,2,2,128,128]{4,3,2,1,0:T(8,128)(2,1)S(1)}, bf16[7,2,2,128,128]{4,3,2,1,0:T(8,128)(2,1)S(1)}, bf1...) custom-call(bf16[7,512]{1,0:T(8,128)(2,1)} %field_ref.1, ...), custom_call_target="tpu_custom_call" | custom-call | tf_op jit(solution)/shard_map/pallas_call | solution.py:248
  1.6 9.7 %all_to_all.5.refs_0_.field_ref = bf16[8,7,512]{2,1,0:T(8,128)(2,1)S(1)} all-to-all(bf16[8,7,512]{2,1,0:T(8,128)(2,1)S(1)} %get-tuple-element.16), channel_id=1, replica_groups=mesh['space'=64,'chaos'=8] {'chaos'}, dimensions={0} | all-to-all | bytes 114688 | tf_op jit(solution)/shard_map/all_to_all | solution.py:257
  11.3 0.6 %shard_map.56 = (f32[8,256]{1,0:T(8,128)S(1)}, f32[8,256]{1,0:T(8,128)S(1)}, bf16[7,2,2,128,128]{4,3,2,1,0:T(8,128)(2,1)S(1)}, bf16[7,2,2,128,128]{4,3,2,1,0:T(8...) custom-call(bf16[8,7,512]{2,1,0:T(8,128)(2,1)S(1)} %all_to_all.5.ref, ...), custom_call_target="tpu_custom_call", output_to_operand_aliasing={{2}: (1, {}), {3}: (2, {}), {4}: (3, {}), {5}: (4, {}), {6}... | custom-call | tf_op jit(solution)/shard_map/pallas_call | solution.py:260
  11.9 4.6 %collective-permute-start = (f32[8,256]{1,0:T(8,128)S(1)}, f32[8,256]{1,0:T(8,128)S(1)}, u32[]{:S(2)}, u32[]{:S(2)}) collective-permute-start(f32[8,256]{1,0:T(8,128)S(1)} %get-tuple-element.25), channel_id=1, source_target_pairs={{8,16},{16,8},{9,17},{17,9},{10,18},{18,10},{11,19},{19,11},{12,20... | collective-permute-start | bytes 24584 | tf_op jit(solution)/shard_map/ppermute | solution.py:292
  16.5 2.2 %collective-permute-start.1 = (f32[8,256]{1,0:T(8,128)S(1)}, f32[8,256]{1,0:T(8,128)S(1)}, u32[]{:S(2)}, u32[]{:S(2)}) collective-permute-start(f32[8,256]{1,0:T(8,128)S(1)} %get-tuple-element.26), channel_id=1, source_target_pairs={{0,8},{8,0},{1,9},{9,1},{2,10},{10,2},{3,11},{11,3},{4,12},{12,4},... | collective-permute-start | bytes 24584 | tf_op jit(solution)/shard_map/ppermute | solution.py:292
  18.8 2.1 %shard_map.57 = f32[7,512]{1,0:T(8,128)S(1)} custom-call(bf16[8,7,512]{2,1,0:T(8,128)(2,1)S(1)} %all_to_all.5.refs_0_.field_ref, bf16[7,4,3,128,128]{4,3,2,1,0:T(8,128)(2,1)} %tiles_hbm.3, bf16[3,112,56]{2,1,0:T(8,128)(2,1)S(1)} %get-tuple-element.23.mixer_ref, f32[32,128]{1,0:T(8,128)S(1)} %get-tuple-element.24.masks_ref, f32[7,512]{1,0:T(8,128)} %rhs_hbm.1), custom_call_target="tpu_custom_call" | custom-call | tf_op jit(solution)/shard_map/pallas_call | solution.py:271
  20.9 2.3 %collective-permute-done = f32[8,256]{1,0:T(8,128)S(1)} collective-permute-done((f32[8,256]{1,0:T(8,128)S(1)}, f32[8,256]{1,0:T(8,128)S(1)}, u32[]{:S(2)}, u32[]{:S(2)}) %collective-permute-start) | collective-permute-done | bytes 8224 | tf_op jit(solution)/shard_map/ppermute | solution.py:292
  23.2 0.0 collective-permute-done.1
  23.2 0.6 %fusion = f32[7,512]{1,0:T(8,128)} fusion(f32[7,512]{1,0:T(8,128)S(1)} %shard_map.57, f32[8,256]{1,0:T(8,128)S(1)} %get-tuple-element.28, f32[8,256]{1,0:T(8,128)S(1)} %get-tuple-element.27), kind=kLoop, calls=%fused_computation.1 | loop fusion | flops 7168 | bytes 45056 | tf_op jit(solution)/shard_map/sub | solution.py:299
  (1 shorter events, 0.0 us)
Async XLA Ops:
  11.9 11.3 %collective-permute-start = (f32[8,256]{1,0:T(8,128)S(1)}, f32[8,256]{1,0:T(8,128)S(1)}, u32[]{:S(2)}, u32[]{:S(2)}) collective-permute-start(f32[8,256]{1,0:T(8,128)S(1)} %get-tuple-element.25), channel_id=1, source_target_pairs={{8,16},{16,8},{9,17},{17,9},{10,18},{18,10},{11,19},{19,11},{12,20... | collective-permute-start | bytes 24584 | tf_op jit(solution)/shard_map/ppermute | solution.py:292
  16.5 6.7 %collective-permute-start.1 = (f32[8,256]{1,0:T(8,128)S(1)}, f32[8,256]{1,0:T(8,128)S(1)}, u32[]{:S(2)}, u32[]{:S(2)}) collective-permute-start(f32[8,256]{1,0:T(8,128)S(1)} %get-tuple-element.26), channel_id=1, source_target_pairs={{0,8},{8,0},{1,9},{9,1},{2,10},{10,2},{3,11},{11,3},{4,12},{12,4},... | collective-permute-start | bytes 24584 | tf_op jit(solution)/shard_map/ppermute | solution.py:292

commit v7 on v6

--- a/solution.py
+++ b/solution.py
@@ -20,6 +20,10 @@
 def is_late():
     upper = lax.rem(lax.axis_index("space") // RUN, 2)
     return lax.axis_index("chaos") // 2 == (1 - upper) * (lax.axis_size("chaos") // 2 - 1)
+
+
+def in_vmem(x):
+    return pltpu.with_memory_space_constraint(x, pltpu.VMEM)
 
 
 def in_hbm(x):
@@ -231,12 +235,12 @@
     side = (terms, REACH, near - 1, size, size)
     side_masks = REACH * (near - 1) * REACH
     staged_shapes = (
-        halves(*side),
-        halves(*side),
-        halves(BLOCKS, 2 * terms * ROWS, chaos),
-        floats(side_masks, size),
-        floats(side_masks, size),
-        floats(tile_rows * (near - 1) * tile_rows, size),
+        pltpu.VMEM(side, jnp.bfloat16),
+        pltpu.VMEM(side, jnp.bfloat16),
+        pltpu.VMEM((BLOCKS, 2 * terms * ROWS, chaos), jnp.bfloat16),
+        pltpu.VMEM((side_masks, size), jnp.float32),
+        pltpu.VMEM((side_masks, size), jnp.float32),
+        pltpu.VMEM((tile_rows * (near - 1) * tile_rows, size), jnp.float32),
     )
     stage_scratch = [
         pltpu.SMEM(offsets.shape, jnp.int32),
@@ -265,7 +269,7 @@
         input_output_aliases={1 + i: 2 + i for i in range(6)},
         scratch_shapes=[*stage_scratch, pltpu.VMEM((2, chaos, REACH * size), jnp.float32)],
         compiler_params=params,
-    )(field, *staged, *sources)
+    )(field, *map(in_vmem, staged), *sources)
     mixer, own_masks = staged[2], staged[5]
 
     main = pl.pallas_call(

time: 24.1 us -> 24.1 us (level)
  no operation moved by 1% of the time
where the time goes in v7:
time: 24.1 us; the launch traced here: 23.9 us
  blocking collectives  9.71 us (40%)
  starting transfers between devices  6.8 us (28%)
  Pallas kernels  4.32 us (18%)
  waiting for transfers between devices  2.35 us (10%)
  other arithmetic  0.62 us (3%)
    all_to_all x1, blocking collectives, body(): field = lax.all_to_all(copies, 'chaos', 0, 0)  9.71 us
    ppermute x2, starting transfers between devices, swap(): lax.ppermute(x, axes, [p for a, b, s in pairs if s % 2 == parity for p in...  6.8 us
    ppermute x2, waiting for transfers between devices, swap(): lax.ppermute(x, axes, [p for a, b, s in pairs if s % 2 == parity for p in...  2.35 us
    pallas_call x1, Pallas kernels, body(): pl.pallas_call(own_kernel, out_shape=floats(own, dofs), in_specs=[vmem, h...  2.12 us
    pallas_call x1, Pallas kernels, body(): pl.pallas_call(stage_kernel, out_shape=(halves(groups, own, dofs), *stage...  1.63 us
    sub x1, other arithmetic, body(): return main - got[:own]  0.61 us
    pallas_call x1, Pallas kernels, body(): pl.pallas_call(halos_kernel, out_shape=(halo, halo, *staged_shapes), in_s...  0.58 us
  transfers between devices with their start and end apart: 2, of which 1 were waited for; matrix products, arithmetic and copies ran while one was open for 0% of the time, Pallas kernels for 9%

profile of v7, /device:TPU:256, one launch (start us, length us, event | category | flops | bytes accessed | tf_op | source)
XLA Modules:
  0.0 23.9 jit_solution(11637414168738200722)
XLA Ops:
  0.0 1.6 %shard_map.55 = (bf16[8,7,512]{2,1,0:T(8,128)(2,1)S(1)}, bf16[7,2,2,128,128]{4,3,2,1,0:T(8,128)(2,1)S(1)}, bf16[7,2,2,128,128]{4,3,2,1,0:T(8,128)(2,1)S(1)}, bf1...) custom-call(bf16[7,512]{1,0:T(8,128)(2,1)} %field_ref.1, ...), custom_call_target="tpu_custom_call" | custom-call | tf_op jit(solution)/shard_map/pallas_call | solution.py:252
  1.6 9.7 %all_to_all.5.refs_0_.field_ref = bf16[8,7,512]{2,1,0:T(8,128)(2,1)S(1)} all-to-all(bf16[8,7,512]{2,1,0:T(8,128)(2,1)S(1)} %get-tuple-element.16), channel_id=1, replica_groups=mesh['space'=64,'chaos'=8] {'chaos'}, dimensions={0} | all-to-all | bytes 114688 | tf_op jit(solution)/shard_map/all_to_all | solution.py:261
  11.3 0.6 %shard_map.56 = (f32[8,256]{1,0:T(8,128)S(1)}, f32[8,256]{1,0:T(8,128)S(1)}, bf16[7,2,2,128,128]{4,3,2,1,0:T(8,128)(2,1)S(1)}, bf16[7,2,2,128,128]{4,3,2,1,0:T(8...) custom-call(bf16[8,7,512]{2,1,0:T(8,128)(2,1)S(1)} %all_to_all.5.ref, ...), custom_call_target="tpu_custom_call", output_to_operand_aliasing={{2}: (1, {}), {3}: (2, {}), {4}: (3, {}), {5}: (4, {}), {6}... | custom-call | tf_op jit(solution)/shard_map/pallas_call | solution.py:264
  11.9 4.6 %collective-permute-start = (f32[8,256]{1,0:T(8,128)S(1)}, f32[8,256]{1,0:T(8,128)S(1)}, u32[]{:S(2)}, u32[]{:S(2)}) collective-permute-start(f32[8,256]{1,0:T(8,128)S(1)} %get-tuple-element.25), channel_id=1, source_target_pairs={{8,16},{16,8},{9,17},{17,9},{10,18},{18,10},{11,19},{19,11},{12,20... | collective-permute-start | bytes 24584 | tf_op jit(solution)/shard_map/ppermute | solution.py:296
  16.5 2.2 %collective-permute-start.1 = (f32[8,256]{1,0:T(8,128)S(1)}, f32[8,256]{1,0:T(8,128)S(1)}, u32[]{:S(2)}, u32[]{:S(2)}) collective-permute-start(f32[8,256]{1,0:T(8,128)S(1)} %get-tuple-element.26), channel_id=1, source_target_pairs={{0,8},{8,0},{1,9},{9,1},{2,10},{10,2},{3,11},{11,3},{4,12},{12,4},... | collective-permute-start | bytes 24584 | tf_op jit(solution)/shard_map/ppermute | solution.py:296
  18.8 2.1 %shard_map.57 = f32[7,512]{1,0:T(8,128)S(1)} custom-call(bf16[8,7,512]{2,1,0:T(8,128)(2,1)S(1)} %all_to_all.5.refs_0_.field_ref, bf16[7,4,3,128,128]{4,3,2,1,0:T(8,128)(2,1)} %tiles_hbm.3, bf16[3,112,56]{2,1,0:T(8,128)(2,1)S(1)} %get-tuple-element.23.mixer_ref, f32[32,128]{1,0:T(8,128)S(1)} %get-tuple-element.24.masks_ref, f32[7,512]{1,0:T(8,128)} %rhs_hbm.1), custom_call_target="tpu_custom_call" | custom-call | tf_op jit(solution)/shard_map/pallas_call | solution.py:275
  20.9 2.3 %collective-permute-done = f32[8,256]{1,0:T(8,128)S(1)} collective-permute-done((f32[8,256]{1,0:T(8,128)S(1)}, f32[8,256]{1,0:T(8,128)S(1)}, u32[]{:S(2)}, u32[]{:S(2)}) %collective-permute-start) | collective-permute-done | bytes 8224 | tf_op jit(solution)/shard_map/ppermute | solution.py:296
  23.2 0.0 collective-permute-done.1
  23.2 0.6 %fusion = f32[7,512]{1,0:T(8,128)} fusion(f32[7,512]{1,0:T(8,128)S(1)} %shard_map.57, f32[8,256]{1,0:T(8,128)S(1)} %get-tuple-element.28, f32[8,256]{1,0:T(8,128)S(1)} %get-tuple-element.27), kind=kLoop, calls=%fused_computation.1 | loop fusion | flops 7168 | bytes 45056 | tf_op jit(solution)/shard_map/sub | solution.py:303
  (1 shorter events, 0.0 us)
Async XLA Ops:
  11.9 11.3 %collective-permute-start = (f32[8,256]{1,0:T(8,128)S(1)}, f32[8,256]{1,0:T(8,128)S(1)}, u32[]{:S(2)}, u32[]{:S(2)}) collective-permute-start(f32[8,256]{1,0:T(8,128)S(1)} %get-tuple-element.25), channel_id=1, source_target_pairs={{8,16},{16,8},{9,17},{17,9},{10,18},{18,10},{11,19},{19,11},{12,20... | collective-permute-start | bytes 24584 | tf_op jit(solution)/shard_map/ppermute | solution.py:296
  16.5 6.7 %collective-permute-start.1 = (f32[8,256]{1,0:T(8,128)S(1)}, f32[8,256]{1,0:T(8,128)S(1)}, u32[]{:S(2)}, u32[]{:S(2)}) collective-permute-start(f32[8,256]{1,0:T(8,128)S(1)} %get-tuple-element.26), channel_id=1, source_target_pairs={{0,8},{8,0},{1,9},{9,1},{2,10},{10,2},{3,11},{11,3},{4,12},{12,4},... | collective-permute-start | bytes 24584 | tf_op jit(solution)/shard_map/ppermute | solution.py:296

commit v8 on v7

--- a/solution.py
+++ b/solution.py
@@ -167,22 +167,29 @@
     field_ref, hbm_refs, halo_refs = refs[0], refs[7:10], refs[10:12]
     staged, scratch, gathered = refs[12:18], refs[18:22], refs[22]
 
+    size = staged[0].shape[3]
+
+    def make_halos(ready):
+        parts = [side_parts(which, field_ref, staged[2], size, gathered.at[which]) for which in range(2)]
+        for which in range(2):
+            ready(which)
+            side_halo(parts[which], staged[which], staged[3 + which], halo_refs[which])
+
     @pl.when(is_late())
     def _():
         for move in moves_of(hbm_refs, staged, scratch):
             move.start()
         stage(hbm_refs, staged, scratch)
 
-    size = staged[0].shape[3]
-    parts = [side_parts(which, field_ref, staged[2], size, gathered.at[which]) for which in range(2)]
-
-    @pl.when(is_late())
+        def ready(which):
+            for move in moves_of(hbm_refs, staged, scratch, 2 + which, 3 + which):
+                move.wait()
+
+        make_halos(ready)
+
+    @pl.when(jnp.logical_not(is_late()))
     def _():
-        for move in moves_of(hbm_refs, staged, scratch, 2):
-            move.wait()
-
-    for which in range(2):
-        side_halo(parts[which], staged[which], staged[3 + which], halo_refs[which])
+        make_halos(lambda which: None)
 
 
 def own_kernel(

time: 24.1 us -> 24.1 us (level)
  no operation moved by 1% of the time
where the time goes in v8:
time: 24.1 us; the launch traced here: 23.8 us
  blocking collectives  9.71 us (40%)
  starting transfers between devices  6.8 us (28%)
  Pallas kernels  4.28 us (18%)
  waiting for transfers between devices  2.35 us (10%)
  other arithmetic  0.62 us (3%)
    all_to_all x1, blocking collectives, body(): field = lax.all_to_all(copies, 'chaos', 0, 0)  9.71 us
    ppermute x2, starting transfers between devices, swap(): lax.ppermute(x, axes, [p for a, b, s in pairs if s % 2 == parity for p in...  6.8 us
    ppermute x2, waiting for transfers between devices, swap(): lax.ppermute(x, axes, [p for a, b, s in pairs if s % 2 == parity for p in...  2.35 us
    pallas_call x1, Pallas kernels, body(): pl.pallas_call(own_kernel, out_shape=floats(own, dofs), in_specs=[vmem, h...  2.12 us
    pallas_call x1, Pallas kernels, body(): pl.pallas_call(stage_kernel, out_shape=(halves(groups, own, dofs), *stage...  1.63 us
    sub x1, other arithmetic, body(): return main - got[:own]  0.61 us
    pallas_call x1, Pallas kernels, body(): pl.pallas_call(halos_kernel, out_shape=(halo, halo, *staged_shapes), in_s...  0.54 us
  transfers between devices with their start and end apart: 2, of which 1 were waited for; matrix products, arithmetic and copies ran while one was open for 0% of the time, Pallas kernels for 9%

profile of v8, /device:TPU:256, one launch (start us, length us, event | category | flops | bytes accessed | tf_op | source)
XLA Modules:
  0.0 23.8 jit_solution(46223018781070348)
XLA Ops:
  0.0 1.6 %shard_map.55 = (bf16[8,7,512]{2,1,0:T(8,128)(2,1)S(1)}, bf16[7,2,2,128,128]{4,3,2,1,0:T(8,128)(2,1)S(1)}, bf16[7,2,2,128,128]{4,3,2,1,0:T(8,128)(2,1)S(1)}, bf1...) custom-call(bf16[7,512]{1,0:T(8,128)(2,1)} %field_ref.1, ...), custom_call_target="tpu_custom_call" | custom-call | tf_op jit(solution)/shard_map/pallas_call | solution.py:259
  1.6 9.7 %all_to_all.5.refs_0_.field_ref = bf16[8,7,512]{2,1,0:T(8,128)(2,1)S(1)} all-to-all(bf16[8,7,512]{2,1,0:T(8,128)(2,1)S(1)} %get-tuple-element.16), channel_id=1, replica_groups=mesh['space'=64,'chaos'=8] {'chaos'}, dimensions={0} | all-to-all | bytes 114688 | tf_op jit(solution)/shard_map/all_to_all | solution.py:268
  11.3 0.5 %shard_map.56 = (f32[8,256]{1,0:T(8,128)S(1)}, f32[8,256]{1,0:T(8,128)S(1)}, bf16[7,2,2,128,128]{4,3,2,1,0:T(8,128)(2,1)S(1)}, bf16[7,2,2,128,128]{4,3,2,1,0:T(8...) custom-call(bf16[8,7,512]{2,1,0:T(8,128)(2,1)S(1)} %all_to_all.5.ref, ...), custom_call_target="tpu_custom_call", output_to_operand_aliasing={{2}: (1, {}), {3}: (2, {}), {4}: (3, {}), {5}: (4, {}), {6}... | custom-call | tf_op jit(solution)/shard_map/pallas_call | solution.py:271
  11.9 4.6 %collective-permute-start = (f32[8,256]{1,0:T(8,128)S(1)}, f32[8,256]{1,0:T(8,128)S(1)}, u32[]{:S(2)}, u32[]{:S(2)}) collective-permute-start(f32[8,256]{1,0:T(8,128)S(1)} %get-tuple-element.25), channel_id=1, source_target_pairs={{8,16},{16,8},{9,17},{17,9},{10,18},{18,10},{11,19},{19,11},{12,20... | collective-permute-start | bytes 24584 | tf_op jit(solution)/shard_map/ppermute | solution.py:303
  16.5 2.2 %collective-permute-start.1 = (f32[8,256]{1,0:T(8,128)S(1)}, f32[8,256]{1,0:T(8,128)S(1)}, u32[]{:S(2)}, u32[]{:S(2)}) collective-permute-start(f32[8,256]{1,0:T(8,128)S(1)} %get-tuple-element.26), channel_id=1, source_target_pairs={{0,8},{8,0},{1,9},{9,1},{2,10},{10,2},{3,11},{11,3},{4,12},{12,4},... | collective-permute-start | bytes 24584 | tf_op jit(solution)/shard_map/ppermute | solution.py:303
  18.7 2.1 %shard_map.57 = f32[7,512]{1,0:T(8,128)S(1)} custom-call(bf16[8,7,512]{2,1,0:T(8,128)(2,1)S(1)} %all_to_all.5.refs_0_.field_ref, bf16[7,4,3,128,128]{4,3,2,1,0:T(8,128)(2,1)} %tiles_hbm.3, bf16[3,112,56]{2,1,0:T(8,128)(2,1)S(1)} %get-tuple-element.23.mixer_ref, f32[32,128]{1,0:T(8,128)S(1)} %get-tuple-element.24.masks_ref, f32[7,512]{1,0:T(8,128)} %rhs_hbm.1), custom_call_target="tpu_custom_call" | custom-call | tf_op jit(solution)/shard_map/pallas_call | solution.py:282
  20.8 2.3 %collective-permute-done = f32[8,256]{1,0:T(8,128)S(1)} collective-permute-done((f32[8,256]{1,0:T(8,128)S(1)}, f32[8,256]{1,0:T(8,128)S(1)}, u32[]{:S(2)}, u32[]{:S(2)}) %collective-permute-start) | collective-permute-done | bytes 8224 | tf_op jit(solution)/shard_map/ppermute | solution.py:303
  23.2 0.0 collective-permute-done.1
  23.2 0.6 %fusion = f32[7,512]{1,0:T(8,128)} fusion(f32[7,512]{1,0:T(8,128)S(1)} %shard_map.57, f32[8,256]{1,0:T(8,128)S(1)} %get-tuple-element.28, f32[8,256]{1,0:T(8,128)S(1)} %get-tuple-element.27), kind=kLoop, calls=%fused_computation.1 | loop fusion | flops 7168 | bytes 45056 | tf_op jit(solution)/shard_map/sub | solution.py:310
  (1 shorter events, 0.0 us)
Async XLA Ops:
  11.9 11.3 %collective-permute-start = (f32[8,256]{1,0:T(8,128)S(1)}, f32[8,256]{1,0:T(8,128)S(1)}, u32[]{:S(2)}, u32[]{:S(2)}) collective-permute-start(f32[8,256]{1,0:T(8,128)S(1)} %get-tuple-element.25), channel_id=1, source_target_pairs={{8,16},{16,8},{9,17},{17,9},{10,18},{18,10},{11,19},{19,11},{12,20... | collective-permute-start | bytes 24584 | tf_op jit(solution)/shard_map/ppermute | solution.py:303
  16.5 6.7 %collective-permute-start.1 = (f32[8,256]{1,0:T(8,128)S(1)}, f32[8,256]{1,0:T(8,128)S(1)}, u32[]{:S(2)}, u32[]{:S(2)}) collective-permute-start(f32[8,256]{1,0:T(8,128)S(1)} %get-tuple-element.26), channel_id=1, source_target_pairs={{0,8},{8,0},{1,9},{9,1},{2,10},{10,2},{3,11},{11,3},{4,12},{12,4},... | collective-permute-start | bytes 24584 | tf_op jit(solution)/shard_map/ppermute | solution.py:303

commit v9 on v8

--- a/solution.py
+++ b/solution.py
@@ -10,7 +10,7 @@
 SPAN = 2 * REACH + 1
 RUN = 4
 ACROSS = (3, 2, 0, 1)
-BLOCKS = 3
+SIDES = 2
 
 
 def across(c):
@@ -51,15 +51,24 @@
     return odd * (tile_rows - REACH), (1 - odd) * (tile_rows - REACH)
 
 
+def set_mixer(mixer_out, galerkin, mixer, owners):
+    terms = galerkin.shape[0]
+    own = galerkin.shape[1] // lax.axis_size("chaos")
+    mixer[...] = jnp.zeros_like(mixer)
+    for b, owner in enumerate(owners):
+        for k in range(terms):
+            mixer[b, k, :own, :] = galerkin[k, pl.ds(owner * own, own), :]
+    parts = split(mixer[...].reshape(len(owners), terms * ROWS, galerkin.shape[1]))
+    mixer_out[...] = jnp.concatenate(parts, axis=1).astype(jnp.bfloat16)
+
+
 def stage(hbm_refs, staged, scratch):
-    _, _, mixer_out, first_masks, second_masks, own_masks = staged
+    _, _, mixer_out, first_masks, second_masks = staged
     offsets, galerkin, mixer, _ = scratch
     moves = moves_of(hbm_refs, staged, scratch, 0, 2)
-    terms, tile_rows, near, _, _ = hbm_refs[1].shape
+    tile_rows, near = hbm_refs[1].shape[1:3]
     groups = lax.axis_size("chaos")
-    own = galerkin.shape[1] // groups
     space, block = lax.axis_index("space"), lax.axis_index("chaos")
-    mixer[...] = jnp.zeros_like(mixer)
     moves[0].wait()
     place = lax.rem(space, RUN)
     at_end = jnp.logical_or(place == 0, place == RUN - 1)
@@ -67,17 +76,13 @@
     for c in range(groups):
         here = jnp.where(place == 0, across(c) == block, c == block)
         far_off = jnp.where(here, jnp.where(place == 0, c, across(c)), far_off)
-    for b, owner in enumerate((jnp.where(at_end, far_off, block), block, block)):
-        for k in range(terms):
-            mixer[b, k, :own, :] = galerkin[k, pl.ds(owner * own, own), :]
-    parts = split(mixer[...].reshape(BLOCKS, terms * ROWS, groups * own))
-    mixer_out[...] = jnp.concatenate(parts, axis=1).astype(jnp.bfloat16)
+    set_mixer(mixer_out, galerkin, mixer, (jnp.where(at_end, far_off, block), block))
     moves[1].wait()
 
     first_row, second_row = side_rows(tile_rows)
 
     def row_of(flag):
-        return jnp.full((1, own_masks.shape[1]), flag.astype(jnp.float32))
+        return jnp.full((1, first_masks.shape[1]), flag.astype(jnp.float32))
 
     for row, out in ((first_row, first_masks), (second_row, second_masks)):
         below = jnp.where(row == 0, -REACH, tile_rows)
@@ -86,20 +91,15 @@
                 for t in range(REACH):
                     at = (i * (near - 1) + s - 1) * REACH + t
                     out[at : at + 1, :] = row_of(row + i + offsets[row + i, s] == below + t)
-    for r in range(tile_rows):
-        for s in range(1, near):
-            for t in range(tile_rows):
-                at = (r * (near - 1) + s - 1) * tile_rows + t
-                own_masks[at : at + 1, :] = row_of(r + offsets[r, s] == t)
 
 
 def stage_kernel(
     field_ref, offsets_hbm, tiles_hbm, galerkin_hbm,
-    copies_out, first_tiles, second_tiles, mixer_out, first_masks, second_masks, own_masks,
+    copies_out, first_tiles, second_tiles, mixer_out, first_masks, second_masks,
     offsets, galerkin, mixer, sems, field, field_sem,
 ):
     hbm_refs = offsets_hbm, tiles_hbm, galerkin_hbm
-    staged = first_tiles, second_tiles, mixer_out, first_masks, second_masks, own_masks
+    staged = first_tiles, second_tiles, mixer_out, first_masks, second_masks
     scratch = offsets, galerkin, mixer, sems
     get_field = pltpu.make_async_copy(field_ref, field, field_sem)
     get_field.start()
@@ -164,8 +164,8 @@
 
 
 def halos_kernel(*refs):
-    field_ref, hbm_refs, halo_refs = refs[0], refs[7:10], refs[10:12]
-    staged, scratch, gathered = refs[12:18], refs[18:22], refs[22]
+    field_ref, hbm_refs, halo_refs = refs[0], refs[6:9], refs[9:11]
+    staged, scratch, gathered = refs[11:16], refs[16:20], refs[20]
 
     size = staged[0].shape[3]
 
@@ -193,31 +193,31 @@
 
 
 def own_kernel(
-    field_ref, tiles_hbm, mixer_ref, masks_ref, rhs_hbm,
-    main_ref, tiles, rhs, gathered, sems,
+    field_ref, offsets_hbm, tiles_hbm, galerkin_hbm, rhs_hbm,
+    main_ref, offsets, tiles, galerkin, rhs, mixer, mixer_parts, gathered, sems,
 ):
     _, tile_rows, near, size, _ = tiles.shape
     own = field_ref.shape[1]
-    get_rhs = pltpu.make_async_copy(rhs_hbm, rhs, sems.at[0])
-    get_tiles = [
-        pltpu.make_async_copy(tiles_hbm.at[:, r], tiles.at[:, r], sems.at[1 + r])
-        for r in range(tile_rows)
-    ]
-    for move in (*get_tiles, get_rhs):
+    pairs = [(galerkin_hbm, galerkin), (offsets_hbm, offsets), (rhs_hbm, rhs)]
+    pairs += [(tiles_hbm.at[:, r], tiles.at[:, r]) for r in range(tile_rows)]
+    moves = [pltpu.make_async_copy(a, b, sems.at[i]) for i, (a, b) in enumerate(pairs)]
+    for move in moves:
         move.start()
-    parts = mix(field_ref, mixer_ref, BLOCKS - 1, slice(None), gathered)
+    moves[0].wait()
+    set_mixer(mixer_parts, galerkin, mixer, (lax.axis_index("chaos"),))
+    parts = mix(field_ref, mixer_parts, 0, slice(None), gathered)
     sums = [jnp.zeros((ROWS, size), jnp.float32) for _ in range(tile_rows)]
+    moves[1].wait()
     for r in range(tile_rows):
-        get_tiles[r].wait()
+        moves[3 + r].wait()
         entries = times_tiles(parts, slice(r * size, (r + 1) * size), tiles[:, r])
         sums[r] += entries[0]
         for s in range(1, near):
             for t in range(tile_rows):
                 if abs(t - r) > REACH or t == r:
                     continue
-                at = (r * (near - 1) + s - 1) * tile_rows + t
-                sums[t] += jnp.where(masks_ref[at : at + 1, :] > 0, entries[s], 0.0)
-    get_rhs.wait()
+                sums[t] += jnp.where(r + offsets[r, s] == t, entries[s], 0.0)
+    moves[2].wait()
     for t in range(tile_rows):
         columns = slice(t * size, (t + 1) * size)
         main_ref[:, columns] = rhs[:, columns] - sums[t][:own]
@@ -244,15 +244,14 @@
     staged_shapes = (
         pltpu.VMEM(side, jnp.bfloat16),
         pltpu.VMEM(side, jnp.bfloat16),
-        pltpu.VMEM((BLOCKS, 2 * terms * ROWS, chaos), jnp.bfloat16),
+        pltpu.VMEM((SIDES, 2 * terms * ROWS, chaos), jnp.bfloat16),
         pltpu.VMEM((side_masks, size), jnp.float32),
         pltpu.VMEM((side_masks, size), jnp.float32),
-        pltpu.VMEM((tile_rows * (near - 1) * tile_rows, size), jnp.float32),
     )
     stage_scratch = [
         pltpu.SMEM(offsets.shape, jnp.int32),
         pltpu.VMEM((terms, chaos, chaos), jnp.float32),
-        pltpu.VMEM((BLOCKS, terms, ROWS, chaos), jnp.float32),
+        pltpu.VMEM((SIDES, terms, ROWS, chaos), jnp.float32),
         pltpu.SemaphoreType.DMA((4,)),
     ]
     sources = in_hbm(offsets), all_tiles, in_hbm(galerkin)
@@ -260,7 +259,7 @@
         stage_kernel,
         out_shape=(halves(groups, own, dofs), *staged_shapes),
         in_specs=[hbm] * 4,
-        out_specs=(vmem,) * 7,
+        out_specs=(vmem,) * 6,
         scratch_shapes=[*stage_scratch, pltpu.VMEM((own, dofs), jnp.bfloat16), pltpu.SemaphoreType.DMA],
         compiler_params=params,
     )(in_hbm(adjoint_field), *sources)
@@ -268,30 +267,32 @@
     field = lax.all_to_all(copies, "chaos", 0, 0)
 
     halo = floats(ROWS, REACH * size)
-    first, second, *staged = pl.pallas_call(
+    first, second, *_ = pl.pallas_call(
         halos_kernel,
         out_shape=(halo, halo, *staged_shapes),
-        in_specs=[vmem] * 7 + [hbm] * 3,
-        out_specs=(vmem,) * 8,
-        input_output_aliases={1 + i: 2 + i for i in range(6)},
-        scratch_shapes=[*stage_scratch, pltpu.VMEM((2, chaos, REACH * size), jnp.float32)],
+        in_specs=[vmem] * 6 + [hbm] * 3,
+        out_specs=(vmem,) * 7,
+        input_output_aliases={1 + i: 2 + i for i in range(5)},
+        scratch_shapes=[*stage_scratch, pltpu.VMEM((SIDES, chaos, REACH * size), jnp.float32)],
         compiler_params=params,
     )(field, *map(in_vmem, staged), *sources)
-    mixer, own_masks = staged[2], staged[5]
-
     main = pl.pallas_call(
         own_kernel,
         out_shape=floats(own, dofs),
-        in_specs=[vmem, hbm, vmem, vmem, hbm],
+        in_specs=[vmem] + [hbm] * 4,
         out_specs=vmem,
         scratch_shapes=[
+            pltpu.SMEM(offsets.shape, jnp.int32),
             pltpu.VMEM(stiffness_tiles.shape, jnp.bfloat16),
+            pltpu.VMEM((terms, chaos, chaos), jnp.float32),
             pltpu.VMEM((own, dofs), jnp.float32),
+            pltpu.VMEM((1, terms, ROWS, chaos), jnp.float32),
+            pltpu.VMEM((1, 2 * terms * ROWS, chaos), jnp.bfloat16),
             pltpu.VMEM((chaos, dofs), jnp.float32),
-            pltpu.SemaphoreType.DMA((1 + tile_rows,)),
+            pltpu.SemaphoreType.DMA((3 + tile_rows,)),
         ],
         compiler_params=params,
-    )(field, all_tiles, mixer, own_masks, rhs)
+    )(field, *sources, rhs)
 
     def partner(s, c):
         return (s + 1) * groups + (across(c) if s % RUN == RUN - 1 else c)

time: 24.1 us -> 24.1 us (level)
  no operation moved by 1% of the time
where the time goes in v9:
time: 24.1 us; the launch traced here: 23.8 us
  blocking collectives  9.71 us (40%)
  starting transfers between devices  6.8 us (28%)
  Pallas kernels  4.4 us (18%)
  waiting for transfers between devices  2.22 us (9%)
  other arithmetic  0.62 us (3%)
    all_to_all x1, blocking collectives, body(): field = lax.all_to_all(copies, 'chaos', 0, 0)  9.71 us
    ppermute x2, starting transfers between devices, swap(): lax.ppermute(x, axes, [p for a, b, s in pairs if s % 2 == parity for p in...  6.8 us
    pallas_call x1, Pallas kernels, body(): pl.pallas_call(own_kernel, out_shape=floats(own, dofs), in_specs=[vmem] +...  2.24 us
    ppermute x2, waiting for transfers between devices, swap(): lax.ppermute(x, axes, [p for a, b, s in pairs if s % 2 == parity for p in...  2.22 us
    pallas_call x1, Pallas kernels, body(): pl.pallas_call(stage_kernel, out_shape=(halves(groups, own, dofs), *stage...  1.63 us
    sub x1, other arithmetic, body(): return main - got[:own]  0.61 us
    pallas_call x1, Pallas kernels, body(): pl.pallas_call(halos_kernel, out_shape=(halo, halo, *staged_shapes), in_s...  0.53 us
  transfers between devices with their start and end apart: 2, of which 1 were waited for; matrix products, arithmetic and copies ran while one was open for 0% of the time, Pallas kernels for 9%

profile of v9, /device:TPU:256, one launch (start us, length us, event | category | flops | bytes accessed | tf_op | source)
XLA Modules:
  0.0 23.8 jit_solution(17838628213916317098)
XLA Ops:
  0.0 1.6 %shard_map.55 = (bf16[8,7,512]{2,1,0:T(8,128)(2,1)S(1)}, bf16[7,2,2,128,128]{4,3,2,1,0:T(8,128)(2,1)S(1)}, bf16[7,2,2,128,128]{4,3,2,1,0:T(8,128)(2,1)S(1)}, bf1...) custom-call(bf16[7,512]{1,0:T(8,128)(2,1)} %field_ref.1, s32[4,3]{1,0:T(4,128)} %refs_6_.1, ...), custom_call_target="tpu_custom_call" | custom-call | tf_op jit(solution)/shard_map/pallas_call | solution.py:258
  1.6 9.7 %all_to_all.5.field_ref.refs_0_ = bf16[8,7,512]{2,1,0:T(8,128)(2,1)S(1)} all-to-all(bf16[8,7,512]{2,1,0:T(8,128)(2,1)S(1)} %get-tuple-element.13), channel_id=1, replica_groups=mesh['space'=64,'chaos'=8] {'chaos'}, dimensions={0} | all-to-all | bytes 114688 | tf_op jit(solution)/shard_map/all_to_all | solution.py:267
  11.3 0.5 %shard_map.57 = (f32[8,256]{1,0:T(8,128)S(1)}, f32[8,256]{1,0:T(8,128)S(1)}, bf16[7,2,2,128,128]{4,3,2,1,0:T(8,128)(2,1)S(1)}, bf16[7,2,2,128,128]{4,3,2,1,0:T(8...) custom-call(bf16[8,7,512]{2,1,0:T(8,128)(2,1)S(1)} %all_to_all.5.fie, ...), custom_call_target="tpu_custom_call", output_to_operand_aliasing={{2}: (1, {}), {3}: (2, {}), {4}: (3, {}), {5}: (4, {}), {6}... | custom-call | tf_op jit(solution)/shard_map/pallas_call | solution.py:270
  11.9 4.6 %collective-permute-start = (f32[8,256]{1,0:T(8,128)S(1)}, f32[8,256]{1,0:T(8,128)S(1)}, u32[]{:S(2)}, u32[]{:S(2)}) collective-permute-start(f32[8,256]{1,0:T(8,128)S(1)} %get-tuple-element.19), channel_id=1, source_target_pairs={{8,16},{16,8},{9,17},{17,9},{10,18},{18,10},{11,19},{19,11},{12,20... | collective-permute-start | bytes 24584 | tf_op jit(solution)/shard_map/ppermute | solution.py:304
  16.5 2.2 %collective-permute-start.1 = (f32[8,256]{1,0:T(8,128)S(1)}, f32[8,256]{1,0:T(8,128)S(1)}, u32[]{:S(2)}, u32[]{:S(2)}) collective-permute-start(f32[8,256]{1,0:T(8,128)S(1)} %get-tuple-element.20), channel_id=1, source_target_pairs={{0,8},{8,0},{1,9},{9,1},{2,10},{10,2},{3,11},{11,3},{4,12},{12,4},... | collective-permute-start | bytes 24584 | tf_op jit(solution)/shard_map/ppermute | solution.py:304
  18.7 2.2 %shard_map.56 = f32[7,512]{1,0:T(8,128)S(1)} custom-call(bf16[8,7,512]{2,1,0:T(8,128)(2,1)S(1)} %all_to_all.5.field_ref.refs_0_, s32[4,3]{1,0:T(4,128)} %refs_6_.1, bf16[7,4,3,128,128]{4,3,2,1,0:T(8,128)(2,1)} %refs_7_.1, f32[7,56,56]{2,1,0:T(8,128)} %refs_8_.1, f32[7,512]{1,0:T(8,128)} %rhs_hbm.1), custom_call_target="tpu_custom_call" | custom-call | tf_op jit(solution)/shard_map/pallas_call | solution.py:279
  21.0 2.2 %collective-permute-done = f32[8,256]{1,0:T(8,128)S(1)} collective-permute-done((f32[8,256]{1,0:T(8,128)S(1)}, f32[8,256]{1,0:T(8,128)S(1)}, u32[]{:S(2)}, u32[]{:S(2)}) %collective-permute-start) | collective-permute-done | bytes 8224 | tf_op jit(solution)/shard_map/ppermute | solution.py:304
  23.2 0.0 collective-permute-done.1
  23.2 0.6 %fusion = f32[7,512]{1,0:T(8,128)} fusion(f32[7,512]{1,0:T(8,128)S(1)} %shard_map.56, f32[8,256]{1,0:T(8,128)S(1)} %get-tuple-element.22, f32[8,256]{1,0:T(8,128)S(1)} %get-tuple-element.21), kind=kLoop, calls=%fused_computation.1 | loop fusion | flops 7168 | bytes 45056 | tf_op jit(solution)/shard_map/sub | solution.py:311
  (1 shorter events, 0.0 us)
Async XLA Ops:
  11.9 11.3 %collective-permute-start = (f32[8,256]{1,0:T(8,128)S(1)}, f32[8,256]{1,0:T(8,128)S(1)}, u32[]{:S(2)}, u32[]{:S(2)}) collective-permute-start(f32[8,256]{1,0:T(8,128)S(1)} %get-tuple-element.19), channel_id=1, source_target_pairs={{8,16},{16,8},{9,17},{17,9},{10,18},{18,10},{11,19},{19,11},{12,20... | collective-permute-start | bytes 24584 | tf_op jit(solution)/shard_map/ppermute | solution.py:304
  16.5 6.7 %collective-permute-start.1 = (f32[8,256]{1,0:T(8,128)S(1)}, f32[8,256]{1,0:T(8,128)S(1)}, u32[]{:S(2)}, u32[]{:S(2)}) collective-permute-start(f32[8,256]{1,0:T(8,128)S(1)} %get-tuple-element.20), channel_id=1, source_target_pairs={{0,8},{8,0},{1,9},{9,1},{2,10},{10,2},{3,11},{11,3},{4,12},{12,4},... | collective-permute-start | bytes 24584 | tf_op jit(solution)/shard_map/ppermute | solution.py:304

commit v10 on v9

--- a/solution.py
+++ b/solution.py
@@ -9,7 +9,7 @@
 REACH = 2
 SPAN = 2 * REACH + 1
 RUN = 4
-ACROSS = (3, 2, 0, 1)
+ACROSS = (3, 2, 1, 0)
 SIDES = 2
 
 

time: 24.1 us -> 24.1 us (level)
  the two profiles are of different devices: /device:TPU:256 before, /device:TPU:264 now
where the time goes in v10:
time: 24.1 us; the launch traced here: 23.9 us
  blocking collectives  8.87 us (37%)
  starting transfers between devices  7.23 us (30%)
  Pallas kernels  4.4 us (18%)
  waiting for transfers between devices  2.69 us (11%)
  other arithmetic  0.62 us (3%)
    all_to_all x1, blocking collectives, body(): field = lax.all_to_all(copies, 'chaos', 0, 0)  8.87 us
    ppermute x2, starting transfers between devices, swap(): lax.ppermute(x, axes, [p for a, b, s in pairs if s % 2 == parity for p in...  7.23 us
    ppermute x2, waiting for transfers between devices, swap(): lax.ppermute(x, axes, [p for a, b, s in pairs if s % 2 == parity for p in...  2.69 us
    pallas_call x1, Pallas kernels, body(): pl.pallas_call(own_kernel, out_shape=floats(own, dofs), in_specs=[vmem] +...  2.24 us
    pallas_call x1, Pallas kernels, body(): pl.pallas_call(stage_kernel, out_shape=(halves(groups, own, dofs), *stage...  1.63 us
    sub x1, other arithmetic, body(): return main - got[:own]  0.61 us
    pallas_call x1, Pallas kernels, body(): pl.pallas_call(halos_kernel, out_shape=(halo, halo, *staged_shapes), in_s...  0.53 us
  transfers between devices with their start and end apart: 2, of which 1 were waited for; matrix products, arithmetic and copies ran while one was open for 0% of the time, Pallas kernels for 9%

profile of v10, /device:TPU:264, one launch (start us, length us, event | category | flops | bytes accessed | tf_op | source)
XLA Modules:
  0.0 23.9 jit_solution(11610803432277975328)
XLA Ops:
  0.0 1.6 %shard_map.55 = (bf16[8,7,512]{2,1,0:T(8,128)(2,1)S(1)}, bf16[7,2,2,128,128]{4,3,2,1,0:T(8,128)(2,1)S(1)}, bf16[7,2,2,128,128]{4,3,2,1,0:T(8,128)(2,1)S(1)}, bf1...) custom-call(bf16[7,512]{1,0:T(8,128)(2,1)} %field_ref.1, s32[4,3]{1,0:T(4,128)} %refs_6_.1, ...), custom_call_target="tpu_custom_call" | custom-call | tf_op jit(solution)/shard_map/pallas_call | solution.py:258
  1.6 8.9 %all_to_all.5.field_ref.refs_0_ = bf16[8,7,512]{2,1,0:T(8,128)(2,1)S(1)} all-to-all(bf16[8,7,512]{2,1,0:T(8,128)(2,1)S(1)} %get-tuple-element.13), channel_id=1, replica_groups=mesh['space'=64,'chaos'=8] {'chaos'}, dimensions={0} | all-to-all | bytes 114688 | tf_op jit(solution)/shard_map/all_to_all | solution.py:267
  10.5 0.5 %shard_map.57 = (f32[8,256]{1,0:T(8,128)S(1)}, f32[8,256]{1,0:T(8,128)S(1)}, bf16[7,2,2,128,128]{4,3,2,1,0:T(8,128)(2,1)S(1)}, bf16[7,2,2,128,128]{4,3,2,1,0:T(8...) custom-call(bf16[8,7,512]{2,1,0:T(8,128)(2,1)S(1)} %all_to_all.5.fie, ...), custom_call_target="tpu_custom_call", output_to_operand_aliasing={{2}: (1, {}), {3}: (2, {}), {4}: (3, {}), {5}: (4, {}), {6}... | custom-call | tf_op jit(solution)/shard_map/pallas_call | solution.py:270
  11.1 5.3 %collective-permute-start = (f32[8,256]{1,0:T(8,128)S(1)}, f32[8,256]{1,0:T(8,128)S(1)}, u32[]{:S(2)}, u32[]{:S(2)}) collective-permute-start(f32[8,256]{1,0:T(8,128)S(1)} %get-tuple-element.19), channel_id=1, source_target_pairs={{8,16},{16,8},{9,17},{17,9},{10,18},{18,10},{11,19},{19,11},{12,20... | collective-permute-start | bytes 24584 | tf_op jit(solution)/shard_map/ppermute | solution.py:304
  16.4 1.9 %collective-permute-start.1 = (f32[8,256]{1,0:T(8,128)S(1)}, f32[8,256]{1,0:T(8,128)S(1)}, u32[]{:S(2)}, u32[]{:S(2)}) collective-permute-start(f32[8,256]{1,0:T(8,128)S(1)} %get-tuple-element.20), channel_id=1, source_target_pairs={{0,8},{8,0},{1,9},{9,1},{2,10},{10,2},{3,11},{11,3},{4,12},{12,4},... | collective-permute-start | bytes 24584 | tf_op jit(solution)/shard_map/ppermute | solution.py:304
  18.3 2.2 %shard_map.56 = f32[7,512]{1,0:T(8,128)S(1)} custom-call(bf16[8,7,512]{2,1,0:T(8,128)(2,1)S(1)} %all_to_all.5.field_ref.refs_0_, s32[4,3]{1,0:T(4,128)} %refs_6_.1, bf16[7,4,3,128,128]{4,3,2,1,0:T(8,128)(2,1)} %refs_7_.1, f32[7,56,56]{2,1,0:T(8,128)} %refs_8_.1, f32[7,512]{1,0:T(8,128)} %rhs_hbm.1), custom_call_target="tpu_custom_call" | custom-call | tf_op jit(solution)/shard_map/pallas_call | solution.py:279
  20.6 2.7 %collective-permute-done = f32[8,256]{1,0:T(8,128)S(1)} collective-permute-done((f32[8,256]{1,0:T(8,128)S(1)}, f32[8,256]{1,0:T(8,128)S(1)}, u32[]{:S(2)}, u32[]{:S(2)}) %collective-permute-start) | collective-permute-done | bytes 8224 | tf_op jit(solution)/shard_map/ppermute | solution.py:304
  23.2 0.0 collective-permute-done.1
  23.3 0.6 %fusion = f32[7,512]{1,0:T(8,128)} fusion(f32[7,512]{1,0:T(8,128)S(1)} %shard_map.56, f32[8,256]{1,0:T(8,128)S(1)} %get-tuple-element.22, f32[8,256]{1,0:T(8,128)S(1)} %get-tuple-element.21), kind=kLoop, calls=%fused_computation.1 | loop fusion | flops 7168 | bytes 45056 | tf_op jit(solution)/shard_map/sub | solution.py:311
  (1 shorter events, 0.0 us)
Async XLA Ops:
  11.1 12.2 %collective-permute-start = (f32[8,256]{1,0:T(8,128)S(1)}, f32[8,256]{1,0:T(8,128)S(1)}, u32[]{:S(2)}, u32[]{:S(2)}) collective-permute-start(f32[8,256]{1,0:T(8,128)S(1)} %get-tuple-element.19), channel_id=1, source_target_pairs={{8,16},{16,8},{9,17},{17,9},{10,18},{18,10},{11,19},{19,11},{12,20... | collective-permute-start | bytes 24584 | tf_op jit(solution)/shard_map/ppermute | solution.py:304
  16.4 6.9 %collective-permute-start.1 = (f32[8,256]{1,0:T(8,128)S(1)}, f32[8,256]{1,0:T(8,128)S(1)}, u32[]{:S(2)}, u32[]{:S(2)}) collective-permute-start(f32[8,256]{1,0:T(8,128)S(1)} %get-tuple-element.20), channel_id=1, source_target_pairs={{0,8},{8,0},{1,9},{9,1},{2,10},{10,2},{3,11},{11,3},{4,12},{12,4},... | collective-permute-start | bytes 24584 | tf_op jit(solution)/shard_map/ppermute | solution.py:304
